TPU v7x, 32 devices: a whole 2x2x4 slice. The times are simulated.
32 devices in a mesh: groups: 2 (over y), ctx: 4 (over z), head: 2 (over x), sub: 2 (over core).
Axes of the slice: x: 2, y: 2, z: 4, core: 2. Of those that a mesh axis runs over, the one named last changes fastest.
Arguments:
- queries: bfloat16 [2048, 64, 128], P(('groups', 'ctx', 'sub'), 'head'), parts along dimension 0, may hold values from -6 to 6
- keys: bfloat16 [2048, 4, 128], P(('groups', 'ctx', 'sub'), 'head'), parts along dimension 0, may hold values from -6 to 6
- values: bfloat16 [2048, 4, 128], P(('groups', 'ctx', 'sub'), 'head'), parts along dimension 0, may hold values from -6 to 6
- grad_out: bfloat16 [2048, 64, 128], P(('groups', 'ctx', 'sub'), 'head'), parts along dimension 0, may hold values from -9 to 9
- row_lse: float32 [2048, 64], P(('groups', 'ctx', 'sub'), 'head'), parts along dimension 0, may hold values from 5.5 to 6.5
- row_delta: float32 [2048, 64], P(('groups', 'ctx', 'sub'), 'head'), parts along dimension 0, may hold values from -24 to 24
- doc_ids: int32 [2048], P(('groups', 'ctx', 'sub')), parts along dimension 0, may hold values from 0 to 3, never falling along the last dimension, each value on 1 to 512 neighbouring positions
- pairs: int32 [16, 2], P('groups'), parts along dimension 0, may hold values from 0 to 7, as said below
Outputs:
- grad_queries: float32 [2048, 64, 128], P(('groups', 'ctx', 'sub'), 'head'), parts along dimension 0
- grad_keys: float32 [2048, 4, 128], P(('groups', 'ctx', 'sub'), 'head'), parts along dimension 0
- grad_values: float32 [2048, 4, 128], P(('groups', 'ctx', 'sub'), 'head'), parts along dimension 0
There are 2 independent parts, one for each index of `groups`. A program takes and returns all parts, laid end to end along the dimension named above; each array names one. Nothing has to cross between parts.
Inputs may be any that keep to these rules, and one draw needn't show every extreme that they name: `pairs`: row c holds two different span indices, neither equal to c. `doc_ids`: never falls along the tokens; every document appears.
All inputs are finite; a program needn't handle non-finite values.
Results may differ from a plain program's by a relative error of at most 0.0046.
Values may be sent and summed in bfloat16 or wider, within the bound.
No kernel may reach another device: no remote copies, remote signals or barrier semaphores. Data moves between devices by JAX's collectives and lax.ppermute only.
A program may use at most 64 MiB of HBM per device.

v0:
```python
import jax
import jax.numpy as jnp
from jax import lax
from jax.sharding import PartitionSpec as P

QH = 64
KVH = 4


def block_terms(query_blk, upstream, log_norm, row_terms, key_blk, value_blk, allowed, factor):
    scores = (
        jnp.einsum("tghd,kgd->tghk", query_blk, key_blk, preferred_element_type=jnp.float32)
        * factor
    )
    probs = jnp.exp(scores - log_norm[..., None])
    if allowed is not None:
        probs = jnp.where(allowed[:, None, None, :], probs, 0.0)
    grad_probs = jnp.einsum(
        "tghd,kgd->tghk", upstream, value_blk, preferred_element_type=jnp.float32
    )
    grad_scores = probs * (grad_probs - row_terms[..., None])
    probs_low = probs.astype(jnp.bfloat16)
    scores_low = grad_scores.astype(jnp.bfloat16)
    grad_val = jnp.einsum("tghk,tghd->kgd", probs_low, upstream, preferred_element_type=jnp.float32)
    grad_key = (
        jnp.einsum("tghk,tghd->kgd", scores_low, query_blk, preferred_element_type=jnp.float32)
        * factor
    )
    grad_query = (
        jnp.einsum("tghk,kgd->tghd", scores_low, key_blk, preferred_element_type=jnp.float32)
        * factor
    )
    return (grad_query, grad_key, grad_val)


def body(queries, keys, values, grad_out, row_lse, row_delta, doc_ids, pairs):
    rows_here = queries.shape[0]
    heads_here = keys.shape[1]
    head_dim = keys.shape[2]
    grouped = QH // KVH
    factor = head_dim ** (-0.5)
    spans = lax.axis_size(("ctx", "sub"))
    stripe = rows_here // spans
    query_blk = queries.reshape(rows_here, heads_here, grouped, head_dim)
    upstream = grad_out.reshape(rows_here, heads_here, grouped, head_dim)
    log_norm = row_lse.reshape(rows_here, heads_here, grouped)
    row_terms = row_delta.reshape(rows_here, heads_here, grouped)
    positions = jnp.arange(rows_here, dtype=jnp.int32)
    allowed = (positions[:, None] >= positions[None, :]) & (doc_ids[:, None] == doc_ids[None, :])
    query_sum, key_local, value_local = block_terms(
        query_blk, upstream, log_norm, row_terms, keys, values, allowed, factor
    )
    stacked = jnp.concatenate([keys, values], axis=2).reshape(rows_here, heads_here * 2 * head_dim)
    features = stacked.shape[1]
    spread = lax.all_to_all(
        stacked.reshape(spans, stripe, features),
        ("ctx", "sub"),
        split_axis=0,
        concat_axis=0,
        tiled=True,
    )
    wanted = jnp.take(spread, pairs.T, axis=0)
    remote = lax.all_to_all(
        wanted, ("ctx", "sub"), split_axis=1, concat_axis=1, tiled=True
    ).reshape(2, rows_here, features)
    remote = remote.reshape(2, rows_here, heads_here, 2 * head_dim)
    returned = []
    for which in range(2):
        far_keys = remote[which, :, :, :head_dim]
        far_values = remote[which, :, :, head_dim:]
        query_part, key_part, value_part = block_terms(
            query_blk, upstream, log_norm, row_terms, far_keys, far_values, None, factor
        )
        query_sum = query_sum + query_part
        returned.append(
            jnp.concatenate([key_part, value_part], axis=2).reshape(rows_here, features)
        )
    outgoing = jnp.stack(returned).reshape(2, spans, stripe, features)
    incoming = lax.all_to_all(outgoing, ("ctx", "sub"), split_axis=1, concat_axis=1, tiled=True)
    owners = pairs.T.reshape(-1)
    select = (jnp.arange(spans, dtype=jnp.int32)[:, None] == owners[None, :]).astype(jnp.float32)
    summed = jnp.dot(
        select,
        incoming.reshape(2 * spans, stripe * features),
        precision=lax.Precision.HIGHEST,
        preferred_element_type=jnp.float32,
    )
    at_home = lax.all_to_all(
        summed.reshape(spans, stripe, features),
        ("ctx", "sub"),
        split_axis=0,
        concat_axis=0,
        tiled=True,
    )
    at_home = at_home.reshape(rows_here, heads_here, 2 * head_dim)
    grad_keys = key_local + at_home[:, :, :head_dim]
    grad_values = value_local + at_home[:, :, head_dim:]
    grad_queries = query_sum.reshape(rows_here, heads_here * grouped, head_dim)
    return (grad_queries, grad_keys, grad_values)


def solution(mesh):
    return jax.shard_map(
        body,
        mesh=mesh,
        in_specs=(
            P(("groups", "ctx", "sub"), "head", None),
            P(("groups", "ctx", "sub"), "head", None),
            P(("groups", "ctx", "sub"), "head", None),
            P(("groups", "ctx", "sub"), "head", None),
            P(("groups", "ctx", "sub"), "head"),
            P(("groups", "ctx", "sub"), "head"),
            P(("groups", "ctx", "sub")),
            P("groups", None),
        ),
        out_specs=(
            P(("groups", "ctx", "sub"), "head", None),
            P(("groups", "ctx", "sub"), "head", None),
            P(("groups", "ctx", "sub"), "head", None),
        ),
        check_vma=False,
    )
```

profile of v0, /device:TPU:0, one launch (start us, length us, event | category | flops | bytes accessed | tf_op | source)
XLA Modules:
  0.0 79.2 jit_solution(9704795043455916158)
XLA Ops:
  0.6 1.1 %pad_maximum_fusion.3 = bf16[128,2,256]{2,1,0:T(2,128)(2,1)S(1)} fusion(bf16[128,2,128]{2,1,0:T(2,128)(2,1)} %param.10, bf16[128,2,128]{2,1,0:T(2,128)(2,1)} %param.9), kind=kLoop, calls=%fused_computation.52 | loop fusion | flops 262144 | bytes 262144 | tf_op jit(solution)/shard_map/concatenate | solution.py:53
  1.7 0.7 reshape_reshape.6
  2.5 6.3 %all-to-all-start = ((bf16[8,16,512]{2,1,0:T(8,128)(2,1)}), bf16[8,16,512]{2,1,0:T(8,128)(2,1)S(1)}, u32[]{:S(2)}, u32[]{:S(2)}) async-start(bf16[8,16,512]{2,1,0:T(8,128)(2,1)} %reshape_reshape.6), calls=%async_computation | async-start | bytes 262144 | tf_op jit(solution)/shard_map/all_to_all | solution.py:55
  8.8 0.7 compare_select_fusion
  9.6 0.7 compare_and_fusion
  10.3 5.3 %all-to-all-done = bf16[8,16,512]{2,1,0:T(8,128)(2,1)S(1)} async-done(((bf16[8,16,512]{2,1,0:T(8,128)(2,1)}), bf16[8,16,512]{2,1,0:T(8,128)(2,1)S(1)}, u32[]{:S(2)}, u32[]{:S(2)}) %all-to-all-start) | async-done | bytes 131104 | tf_op jit(solution)/shard_map/all_to_all | solution.py:55
  15.6 0.6 gather_fusion
  16.3 0.7 copy.137
  17.0 3.4 %all-to-all-start.1 = ((bf16[2,8,16,512]{3,2,0,1:T(8,128)(2,1)}), bf16[2,8,16,512]{3,2,0,1:T(8,128)(2,1)S(1)}, u32[]{:S(2)}, u32[]{:S(2)}) async-start(bf16[2,8,16,512]{3,2,0,1:T(8,128)(2,1)} %copy.137), calls=%async_computation.1 | async-start | bytes 524288 | tf_op jit(solution)/shard_map/all_to_all | solution.py:63
  20.4 1.0 %copy.153 = bf16[128,2,16,128]{0,3,2,1:T(8,128)(2,1)S(1)} copy(bf16[128,2,16,128]{3,2,1,0:T(8,128)(2,1)S(1)} %bitcast.181) | data formatting | bytes 2097152 | tf_op jit(solution)/shard_map/reshape | solution.py:44
  21.4 1.0 %copy.156 = bf16[128,2,16,128]{0,3,2,1:T(8,128)(2,1)S(1)} copy(bf16[128,2,16,128]{3,2,1,0:T(8,128)(2,1)S(1)} %bitcast.174) | data formatting | bytes 2097152 | tf_op jit(solution)/shard_map/reshape | solution.py:45
  22.4 0.7 eq.36
  23.1 0.7 fusion.35
  23.8 6.3 %all-to-all-done.1 = bf16[2,8,16,512]{3,2,0,1:T(8,128)(2,1)S(1)} async-done(((bf16[2,8,16,512]{3,2,0,1:T(8,128)(2,1)}), bf16[2,8,16,512]{3,2,0,1:T(8,128)(2,1)S(1)}, u32[]{:S(2)}, u32[]{:S(2)}) %all-to-all-start.1) | async-done | bytes 262176 | tf_op jit(solution)/shard_map/all_to_all | solution.py:63
  30.1 0.7 copy.138
  30.8 1.0 %reshape_reshape.7 = bf16[2,128,2,256]{3,2,1,0:T(2,128)(2,1)S(1)} reshape(bf16[2,8,16,512]{3,2,1,0:T(8,128)(2,1)} %copy.138) | data formatting | bytes 524288 | tf_op jit(solution)/shard_map/reshape;reshape | solution.py:66
  31.8 0.8 %fusion.48 = (bf16[1,128,2,128]{3,2,1,0:T(2,128)(2,1)S(1)}, bf16[1,128,2,128]{3,2,1,0:T(2,128)(2,1)S(1)}, bf16[1,128,2,128]{3,2,1,0:T(2,128)(2,1)}, bf16[1,128,2,128]{3,2,1,0:T(2,128)(2,1)S(1)}) fusion(bf16[2,128,2,256]{3,2,1,0:T(2,128)(2,1)S(1)} %reshape_reshape.7), kind=kLoop, calls=%fused_computation.75 | loop fusion | bytes 524288 | tf_op jit(solution)/shard_map/slice | solution.py:70
  32.6 0.4 fusion.38
  33.1 1.0 %fusion.1 = bf16[128,2,16,128]{0,3,2,1:T(8,128)(2,1)S(1)} fusion(f32[2,128,128,16]{2,1,3,0:T(8,128)S(1)} %fusion.38, f32[128,2,16]{0,2,1:T(8,128)S(1)} %bitcast.190, f32[128,2,16]{0,2,1:T(8,128)S(1)} %bitcast.184, bf16[128,2,16,128]{3,2,1,0:T(8,128)(2,1)S(1)} %bitcast.175, bf16[1,128,2,128]{3,2,1,0:T(2,128)(2,1)S(1)} %get-tuple-element.17), kind=kOutput, calls=%fused_computation.4 | convolution fusion | flops 136839168 | bytes 4292608 | tf_op jit(solution)/shard_map/tghd,kgd->tghk/dot_general | solution.py:18
  34.0 0.4 fusion.13
  34.5 0.5 convolution_bitcast_fusion.1
  35.3 0.9 %stack.8 = f32[1,8,16,512]{3,2,1,0:T(8,128)} reshape(f32[128,2,256]{2,1,0:T(2,128)S(1)} %copy.165) | data formatting | bytes 524288 | tf_op jit(solution)/shard_map/stack | solution.py:78
  36.2 0.4 fusion.36
  36.6 0.5 convolution_bitcast_fusion.3
  37.1 0.3 copy-done.13
  37.4 0.9 %fusion.4 = bf16[128,2,16,128]{0,3,2,1:T(8,128)(2,1)S(1)} fusion(f32[2,128,128,16]{2,1,3,0:T(8,128)S(1)} %fusion.36, f32[128,2,16]{0,2,1:T(8,128)S(1)} %bitcast.191, f32[128,2,16]{0,2,1:T(8,128)S(1)} %bitcast.187, bf16[128,2,16,128]{3,2,1,0:T(8,128)(2,1)S(1)} %bitcast.176, bf16[1,128,2,128]{3,2,1,0:T(2,128)(2,1)S(1)} %copy-done.13), kind=kOutput, calls=%fused_computation.10 | convolution fusion | flops 136839168 | bytes 4292608 | tf_op jit(solution)/shard_map/tghd,kgd->tghk/dot_general | solution.py:18
  38.4 1.0 %copy-done.6 = bf16[128,2,16,128]{0,3,2,1:T(8,128)(2,1)} copy-done((bf16[128,2,16,128]{0,3,2,1:T(8,128)(2,1)}, bf16[128,2,16,128]{0,3,2,1:T(8,128)(2,1)S(1)}, u32[]{:S(2)}) %copy-start.6) | copy-done | bytes 1048600
  39.4 0.4 fusion.15
  40.1 0.2 stack.7
  40.4 0.8 %copy.166 = f32[2,8,16,512]{3,2,0,1:T(8,128)} copy(f32[2,8,16,512]{3,2,1,0:T(8,128)S(1)} %pad_maximum_fusion) | data formatting | bytes 1048576 | tf_op jit(solution)/shard_map/stack | solution.py:78
  41.2 3.6 %all-to-all-start.2 = ((f32[2,8,16,512]{3,2,0,1:T(8,128)}), f32[2,8,16,512]{3,2,0,1:T(8,128)S(1)}, u32[]{:S(2)}, u32[]{:S(2)}) async-start(f32[2,8,16,512]{3,2,0,1:T(8,128)} %copy.166), calls=%async_computation.2 | async-start | bytes 1048576 | tf_op jit(solution)/shard_map/all_to_all | solution.py:79
  44.9 0.5 fusion.9
  45.4 0.7 fusion.7
  46.1 0.7 copy-done.1
  46.8 1.0 %copy-done.4 = bf16[128,2,16,128]{0,3,2,1:T(8,128)(2,1)} copy-done((bf16[128,2,16,128]{0,3,2,1:T(8,128)(2,1)}, bf16[128,2,16,128]{0,3,2,1:T(8,128)(2,1)S(1)}, u32[]{:S(2)}) %copy-start.4) | copy-done | bytes 1048600
  47.8 1.8 %fusion.39 = f32[2,128,16,128]{1,3,2,0:T(8,128)} fusion(bf16[128,2,16,128]{0,3,2,1:T(8,128)(2,1)S(1)} %fusion.7, bf16[128,2,128,1]{2,1,0,3:T(2,128)(2,1)S(1)} %bitcast.183), kind=kOutput, calls=%fused_computation.63 | convolution fusion | flops 134217728 | bytes 3211264 | tf_op jit(solution)/shard_map/tghk,kgd->tghd/dot_general | solution.py:30
  49.6 10.5 %all-to-all-done.2 = f32[2,8,16,512]{3,2,0,1:T(8,128)S(1)} async-done(((f32[2,8,16,512]{3,2,0,1:T(8,128)}), f32[2,8,16,512]{3,2,0,1:T(8,128)S(1)}, u32[]{:S(2)}, u32[]{:S(2)}) %all-to-all-start.2) | async-done | bytes 524320 | tf_op jit(solution)/shard_map/all_to_all | solution.py:79
  60.2 0.6 fusion.31
  60.8 0.9 %copy.169 = f32[8,16,512]{2,1,0:T(8,128)} copy(f32[8,16,512]{2,0,1:T(8,128)S(1)} %fusion.31) | data formatting | bytes 524288 | tf_op jit(solution)/shard_map/dot_general | solution.py:82
  61.7 3.6 %all-to-all-start.3 = ((f32[8,16,512]{2,1,0:T(8,128)}), f32[8,16,512]{2,1,0:T(8,128)S(1)}, u32[]{:S(2)}, u32[]{:S(2)}) async-start(f32[8,16,512]{2,1,0:T(8,128)} %copy.169), calls=%async_computation.3 | async-start | bytes 524288 | tf_op jit(solution)/shard_map/all_to_all | solution.py:88
  65.3 1.8 %fusion.37 = f32[2,128,128,16]{2,1,3,0:T(8,128)S(1)} fusion(bf16[128,2,16,128]{0,3,2,1:T(8,128)(2,1)} %copy-done.6, bf16[1,128,2,128]{3,2,1,0:T(2,128)(2,1)S(1)} %get-tuple-element.20), kind=kOutput, calls=%fused_computation.61 | convolution fusion | flops 134217728 | bytes 3211264 | tf_op jit(solution)/shard_map/tghk,kgd->tghd/dot_general | solution.py:30
  67.2 2.0 %bitcast_add_fusion = f32[128,2,16,128]{0,3,2,1:T(8,128)} fusion(f32[2,128,128,16]{2,1,3,0:T(8,128)S(1)} %fusion.37, f32[2,128,16,128]{1,3,2,0:T(8,128)S(1)} %copy-done.7, bf16[128,2,16,128]{0,3,2,1:T(8,128)(2,1)S(1)} %copy-done.3, bf16[1,128,2,128]{3,2,1,0:T(2,128)(2,1)S(1)} %get-tuple-element.18), kind=kOutput, calls=%fused_computation.1 | convolution fusion | flops 136839168 | bytes 7405568 | tf_op jit(solution)/shard_map/tghk,kgd->tghd/dot_general | solution.py:30
  69.2 3.0 %copy.173 = f32[128,32,128]{2,1,0:T(8,128)} copy(f32[128,32,128]{0,2,1:T(8,128)} %bitcast.179) | data formatting | bytes 4194304
  72.2 2.5 %all-to-all-done.3 = f32[8,16,512]{2,1,0:T(8,128)S(1)} async-done(((f32[8,16,512]{2,1,0:T(8,128)}), f32[8,16,512]{2,1,0:T(8,128)S(1)}, u32[]{:S(2)}, u32[]{:S(2)}) %all-to-all-start.3) | async-done | bytes 262176 | tf_op jit(solution)/shard_map/all_to_all | solution.py:88
  75.0 2.2 %fusion.19 = f32[128,2,128]{2,0,1:T(8,128)S(1)} fusion(f32[128,2,16,128]{0,3,2,1:T(8,128)} %copy-done.1, bf16[128,2,16,128]{3,2,1,0:T(8,128)(2,1)S(1)} %bitcast.178, f32[128,2,128]{2,1,0:T(2,128)S(1)} %get-tuple-element.15), kind=kOutput, calls=%fused_computation.34 | convolution fusion | flops 134774784 | bytes 3407872 | tf_op jit(solution)/shard_map/tghk,tghd->kgd/dot_general | solution.py:24
  77.3 0.8 copy.175
  78.0 0.4 fusion.18
  78.5 0.8 copy.174
  (49 shorter events, 1.1 us)
Async XLA Ops:
  0.6 19.8 %copy-start.8 = (bf16[128,32,128]{2,1,0:T(8,128)(2,1)S(1)}, bf16[128,32,128]{2,1,0:T(8,128)(2,1)}, u32[]{:S(2)}) copy-start(bf16[128,32,128]{2,1,0:T(8,128)(2,1)} %param.8) | copy-start | bytes 3145732
  2.5 13.1 %all-to-all-start = ((bf16[8,16,512]{2,1,0:T(8,128)(2,1)}), bf16[8,16,512]{2,1,0:T(8,128)(2,1)S(1)}, u32[]{:S(2)}, u32[]{:S(2)}) async-start(bf16[8,16,512]{2,1,0:T(8,128)(2,1)} %reshape_reshape.6), calls=%async_computation | async-start | bytes 262144 | tf_op jit(solution)/shard_map/all_to_all | solution.py:55
  10.3 11.2 %copy-start = (bf16[128,32,128]{2,1,0:T(8,128)(2,1)S(1)}, bf16[128,32,128]{2,1,0:T(8,128)(2,1)}, u32[]{:S(2)}) copy-start(bf16[128,32,128]{2,1,0:T(8,128)(2,1)} %param.11) | copy-start | bytes 3145732
  17.0 13.1 %all-to-all-start.1 = ((bf16[2,8,16,512]{3,2,0,1:T(8,128)(2,1)}), bf16[2,8,16,512]{3,2,0,1:T(8,128)(2,1)S(1)}, u32[]{:S(2)}, u32[]{:S(2)}) async-start(bf16[2,8,16,512]{3,2,0,1:T(8,128)(2,1)} %copy.137), calls=%async_computation.1 | async-start | bytes 524288 | tf_op jit(solution)/shard_map/all_to_all | solution.py:63
  20.4 2.0 %copy-start.19 = (s32[8,2]{0,1:T(2,128)S(1)}, s32[8,2]{0,1:T(2,128)}, u32[]{:S(2)}) copy-start(s32[8,2]{0,1:T(2,128)} %param.15) | copy-start | bytes 196
  20.4 2.7 %copy-start.18 = (s32[128]{0:T(128)S(1)}, s32[128]{0:T(128)}, u32[]{:S(2)}) copy-start(s32[128]{0:T(128)} %param.14) | copy-start | bytes 1540
  30.8 2.3 %copy-start.11 = (f32[128,32]{0,1:T(8,128)S(1)}, f32[128,32]{0,1:T(8,128)}, u32[]{:S(2)}) copy-start(f32[128,32]{0,1:T(8,128)} %param.12) | copy-start | bytes 49156
  31.8 1.3 %copy-start.14 = (f32[128,32]{0,1:T(8,128)S(1)}, f32[128,32]{0,1:T(8,128)}, u32[]{:S(2)}) copy-start(f32[128,32]{0,1:T(8,128)} %param.13) | copy-start | bytes 49156
  34.0 1.0 %copy-start.2 = (bf16[128,2,16,128]{0,3,2,1:T(8,128)(2,1)}, bf16[128,2,16,128]{0,3,2,1:T(8,128)(2,1)S(1)}, u32[]{:S(2)}) copy-start(bf16[128,2,16,128]{0,3,2,1:T(8,128)(2,1)S(1)} %fusion.1) | copy-start | bytes 3145732
  36.6 0.8 %copy-start.13 = (bf16[1,128,2,128]{3,2,1,0:T(2,128)(2,1)S(1)}, bf16[1,128,2,128]{3,2,1,0:T(2,128)(2,1)}, u32[]{:S(2)}) copy-start(bf16[1,128,2,128]{3,2,1,0:T(2,128)(2,1)} %get-tuple-element.19) | copy-start | bytes 196612
  36.6 0.8 %copy-start.15 = (f32[128,32]{0,1:T(8,128)S(1)}, f32[128,32]{0,1:T(8,128)}, u32[]{:S(2)}) copy-start(f32[128,32]{0,1:T(8,128)} %param.13) | copy-start | bytes 49156
  38.4 1.0 %copy-start.6 = (bf16[128,2,16,128]{0,3,2,1:T(8,128)(2,1)}, bf16[128,2,16,128]{0,3,2,1:T(8,128)(2,1)S(1)}, u32[]{:S(2)}) copy-start(bf16[128,2,16,128]{0,3,2,1:T(8,128)(2,1)S(1)} %fusion.4) | copy-start | bytes 3145732
  39.4 0.9 %copy-start.9 = (f32[1,8,16,512]{3,2,1,0:T(8,128)S(1)}, f32[1,8,16,512]{3,2,1,0:T(8,128)}, u32[]{:S(2)}) copy-start(f32[1,8,16,512]{3,2,1,0:T(8,128)} %stack.8) | copy-start | bytes 786436
  39.8 5.0 %copy-start.10 = (bf16[128,2,128]{2,1,0:T(2,128)(2,1)S(1)}, bf16[128,2,128]{2,1,0:T(2,128)(2,1)}, u32[]{:S(2)}) copy-start(bf16[128,2,128]{2,1,0:T(2,128)(2,1)} %param.9) | copy-start | bytes 196612
  39.9 5.0 %copy-start.17 = (pred[128,128]{0,1:T(8,128)(4,1)S(1)}, pred[128,128]{0,1:T(8,128)(4,1)}, u32[]{:S(2)}) copy-start(pred[128,128]{0,1:T(8,128)(4,1)} %fusion.35) | copy-start | bytes 49156
  41.2 4.2 %copy-start.12 = (bf16[128,2,128]{2,1,0:T(2,128)(2,1)S(1)}, bf16[128,2,128]{2,1,0:T(2,128)(2,1)}, u32[]{:S(2)}) copy-start(bf16[128,2,128]{2,1,0:T(2,128)(2,1)} %param.10) | copy-start | bytes 196612
  41.2 4.2 %copy-start.16 = (f32[128,32]{0,1:T(8,128)S(1)}, f32[128,32]{0,1:T(8,128)}, u32[]{:S(2)}) copy-start(f32[128,32]{0,1:T(8,128)} %param.13) | copy-start | bytes 49156
  41.2 18.9 %all-to-all-start.2 = ((f32[2,8,16,512]{3,2,0,1:T(8,128)}), f32[2,8,16,512]{3,2,0,1:T(8,128)S(1)}, u32[]{:S(2)}, u32[]{:S(2)}) async-start(f32[2,8,16,512]{3,2,0,1:T(8,128)} %copy.166), calls=%async_computation.2 | async-start | bytes 1048576 | tf_op jit(solution)/shard_map/all_to_all | solution.py:79
  45.4 1.4 %copy-start.1 = (f32[128,2,16,128]{0,3,2,1:T(8,128)}, f32[128,2,16,128]{0,3,2,1:T(8,128)S(1)}, u32[]{:S(2)}) copy-start(f32[128,2,16,128]{0,3,2,1:T(8,128)S(1)} %fusion.9) | copy-start | bytes 6291460
  46.8 1.0 %copy-start.4 = (bf16[128,2,16,128]{0,3,2,1:T(8,128)(2,1)}, bf16[128,2,16,128]{0,3,2,1:T(8,128)(2,1)S(1)}, u32[]{:S(2)}) copy-start(bf16[128,2,16,128]{0,3,2,1:T(8,128)(2,1)S(1)} %fusion.7) | copy-start | bytes 3145732
  47.8 12.4 %copy-start.20 = (s32[16]{0:T(128)S(1)}, s32[16]{0:T(128)}, u32[]{:S(2)}) copy-start(s32[16]{0:T(128)} %eq.36) | copy-start | bytes 196
  60.8 6.3 %copy-start.3 = (bf16[128,2,16,128]{0,3,2,1:T(8,128)(2,1)S(1)}, bf16[128,2,16,128]{0,3,2,1:T(8,128)(2,1)}, u32[]{:S(2)}) copy-start(bf16[128,2,16,128]{0,3,2,1:T(8,128)(2,1)} %copy-done.2) | copy-start | bytes 3145732
  61.7 13.1 %all-to-all-start.3 = ((f32[8,16,512]{2,1,0:T(8,128)}), f32[8,16,512]{2,1,0:T(8,128)S(1)}, u32[]{:S(2)}, u32[]{:S(2)}) async-start(f32[8,16,512]{2,1,0:T(8,128)} %copy.169), calls=%async_computation.3 | async-start | bytes 524288 | tf_op jit(solution)/shard_map/all_to_all | solution.py:88
  65.3 1.9 %copy-start.7 = (f32[2,128,16,128]{1,3,2,0:T(8,128)S(1)}, f32[2,128,16,128]{1,3,2,0:T(8,128)}, u32[]{:S(2)}) copy-start(f32[2,128,16,128]{1,3,2,0:T(8,128)} %fusion.39) | copy-start | bytes 6291460
  74.9 3.1 %copy-start.5 = (bf16[128,2,16,128]{0,3,2,1:T(8,128)(2,1)S(1)}, bf16[128,2,16,128]{0,3,2,1:T(8,128)(2,1)}, u32[]{:S(2)}) copy-start(bf16[128,2,16,128]{0,3,2,1:T(8,128)(2,1)} %copy-done.4) | copy-start | bytes 3145732
where the time goes:
time: 79.9 us; the launch traced here: 79.2 us
  waiting for transfers between devices  24.7 us (31%)
  local copies, waits for them, and re-layouts  18.5 us (23%)
  starting transfers between devices  17 us (21%)
  matrix products  14.8 us (19%)
  other arithmetic  3.33 us (4%)
  between operations  1.07 us (1%)
    all_to_all x1, waiting for transfers between devices, body(): lax.all_to_all(outgoing, ('ctx', 'sub'), split_axis=1, concat_axis=1, til...  10.5 us
    unnamed x45, local copies, waits for them, and re-layouts  7.62 us
    all_to_all x1, starting transfers between devices, body(): lax.all_to_all(stacked.reshape(spans, stripe, features), ('ctx', 'sub'),...  6.33 us
    all_to_all x1, waiting for transfers between devices, body(): lax.all_to_all(wanted, ('ctx', 'sub'), split_axis=1, concat_axis=1, tiled...  6.28 us
    dot_general x3, matrix products, block_terms(): jnp.einsum('tghk,kgd->tghd', scores_low, key_blk, preferred_element_type=...  5.67 us
    all_to_all x1, waiting for transfers between devices, body(): lax.all_to_all(stacked.reshape(spans, stripe, features), ('ctx', 'sub'),...  5.32 us
    all_to_all x1, starting transfers between devices, body(): lax.all_to_all(outgoing, ('ctx', 'sub'), split_axis=1, concat_axis=1, til...  3.62 us
    all_to_all x1, starting transfers between devices, body(): lax.all_to_all(summed.reshape(spans, stripe, features), ('ctx', 'sub'), s...  3.59 us
  transfers between devices with their start and end apart: 4, of which 4 were waited for; matrix products, arithmetic and copies ran while one was open for 19% of the time, Pallas kernels for 0%

commit v1 on v0

v1 whole, which is shorter than its diff:
```python
import functools

import jax
import jax.numpy as jnp
from jax import lax
from jax.experimental import pallas as pl
from jax.experimental.pallas import tpu as pltpu
from jax.sharding import PartitionSpec as P

QH = 64
KVH = 4
LOG2E = 1.4426950408889634
ROWS = 512
VMEM_LIMIT = 24 * 1024 * 1024


def rows_dot(left, right):
    return lax.dot_general(left, right, (((1,), (1,)), ((), ())), preferred_element_type=jnp.float32)


def tile_terms(key_blk, value_blk, query_blk, upstream, log_norm, row_terms, allowed, factor):
    scores = rows_dot(key_blk, query_blk)
    probs = jnp.exp2(scores * (factor * LOG2E) - log_norm * LOG2E)
    if allowed is not None:
        probs = jnp.where(allowed, probs, 0.0)
    grad_probs = rows_dot(value_blk, upstream)
    grad_scores = probs * (grad_probs - row_terms)
    return probs.astype(jnp.bfloat16), grad_scores.astype(jnp.bfloat16)


def chunks(query_ref, rows):
    tokens, grouped, head_dim = query_ref.shape
    step = rows // grouped
    return [(i, slice(i * step, (i + 1) * step), slice(i * rows, (i + 1) * rows)) for i in range(tokens // step)]


def local_kernel(factor, rows, kv_ref, query_ref, up_ref, norm_ref, term_ref, docs_ref, doc_col_ref,
                 dkv_ref, dq_ref):
    tokens, grouped, head_dim = query_ref.shape
    key_blk, value_blk = kv_ref[0, 0], kv_ref[1, 0]
    grad_key = jnp.zeros((tokens, head_dim), jnp.float32)
    grad_val = jnp.zeros((tokens, head_dim), jnp.float32)
    for i, toks, cols in chunks(query_ref, rows):
        query_blk = query_ref[toks].reshape(rows, head_dim)
        upstream = up_ref[toks].reshape(rows, head_dim)
        position = lax.broadcasted_iota(jnp.int32, (tokens, rows), 1) // grouped + toks.start
        allowed = (lax.broadcasted_iota(jnp.int32, (tokens, rows), 0) <= position) & (
            doc_col_ref[...] == docs_ref[:, cols]
        )
        probs, grads = tile_terms(
            key_blk, value_blk, query_blk, upstream, norm_ref[0, :, cols], term_ref[0, :, cols], allowed, factor
        )
        grad_val += jnp.dot(probs, upstream, preferred_element_type=jnp.float32)
        grad_key += jnp.dot(grads, query_blk, preferred_element_type=jnp.float32)
        grad_query = lax.dot_general(
            grads, key_blk, (((0,), (0,)), ((), ())), preferred_element_type=jnp.float32
        )
        dq_ref[toks] = (grad_query * factor).reshape(rows // grouped, grouped, head_dim)
    dkv_ref[0, 0] = grad_key * factor
    dkv_ref[1, 0] = grad_val


def listed_kernel(factor, rows, index_ref, one_ref, two_ref, query_ref, up_ref, norm_ref, term_ref, dkv_ref):
    tokens, grouped, head_dim = query_ref.shape
    key_blk = jnp.concatenate([one_ref[0, 0, 0], two_ref[0, 0, 0]], axis=0)
    value_blk = jnp.concatenate([one_ref[0, 1, 0], two_ref[0, 1, 0]], axis=0)
    grad_key = jnp.zeros((2 * tokens, head_dim), jnp.float32)
    grad_val = jnp.zeros((2 * tokens, head_dim), jnp.float32)
    for i, toks, cols in chunks(query_ref, rows):
        query_blk = query_ref[toks].reshape(rows, head_dim)
        upstream = up_ref[toks].reshape(rows, head_dim)
        probs, grads = tile_terms(
            key_blk, value_blk, query_blk, upstream, norm_ref[0, :, cols], term_ref[0, :, cols], None, factor
        )
        grad_val += jnp.dot(probs, upstream, preferred_element_type=jnp.float32)
        grad_key += jnp.dot(grads, query_blk, preferred_element_type=jnp.float32)
    grad_key = (grad_key * factor).astype(dkv_ref.dtype)
    grad_val = grad_val.astype(dkv_ref.dtype)
    for which in range(2):
        dkv_ref[which, 0, 0] = grad_key[which * tokens:(which + 1) * tokens]
        dkv_ref[which, 1, 0] = grad_val[which * tokens:(which + 1) * tokens]


def query_kernel(factor, rows, index_ref, one_ref, two_ref, query_ref, up_ref, norm_ref, term_ref, near_ref, dq_ref):
    tokens, grouped, head_dim = query_ref.shape
    key_blk = jnp.concatenate([one_ref[0, 0, 0], two_ref[0, 0, 0]], axis=0)
    value_blk = jnp.concatenate([one_ref[0, 1, 0], two_ref[0, 1, 0]], axis=0)
    for i, toks, cols in chunks(query_ref, rows):
        query_blk = query_ref[toks].reshape(rows, head_dim)
        upstream = up_ref[toks].reshape(rows, head_dim)
        probs, grads = tile_terms(
            key_blk, value_blk, query_blk, upstream, norm_ref[0, :, cols], term_ref[0, :, cols], None, factor
        )
        grad_query = lax.dot_general(
            grads, key_blk, (((0,), (0,)), ((), ())), preferred_element_type=jnp.float32
        )
        dq_ref[toks] = near_ref[toks] + (grad_query * factor).reshape(rows // grouped, grouped, head_dim)


def body(queries, keys, values, grad_out, row_lse, row_delta, doc_ids, pairs):
    tokens, heads, head_dim = queries.shape
    kv_heads = keys.shape[1]
    grouped = QH // KVH
    factor = head_dim ** (-0.5)
    ring = lax.axis_size("ctx")
    subs = lax.axis_size("sub")
    ctx = lax.axis_index("ctx")
    sub = lax.axis_index("sub")
    rows = min(ROWS, tokens * grouped)
    cols = tokens * grouped

    kv = jnp.stack([keys, values]).transpose(0, 2, 1, 3)
    norm = row_lse.reshape(tokens, kv_heads, grouped).transpose(1, 0, 2).reshape(kv_heads, 1, cols)
    term = row_delta.reshape(tokens, kv_heads, grouped).transpose(1, 0, 2).reshape(kv_heads, 1, cols)
    docs = jnp.repeat(doc_ids, grouped).reshape(1, cols)
    doc_col = doc_ids.reshape(tokens, 1)

    gathered = lax.all_gather(kv, ("ctx", "sub"), axis=0, tiled=False)
    index = lax.dynamic_index_in_dim(pairs, ctx * subs + sub, 0, keepdims=False)

    params = pltpu.CompilerParams(vmem_limit_bytes=VMEM_LIMIT, dimension_semantics=("arbitrary",))
    row_spec = lambda g, *_: (0, g, 0)
    lane_spec = lambda g, *_: (g, 0, 0)
    query_specs = [
        pl.BlockSpec((tokens, grouped, head_dim), row_spec),
        pl.BlockSpec((tokens, grouped, head_dim), row_spec),
        pl.BlockSpec((1, 1, cols), lane_spec),
        pl.BlockSpec((1, 1, cols), lane_spec),
    ]
    work = 2 * tokens * tokens * heads * head_dim
    moved = 2 * queries.size * 2

    near_kv, near_query = pl.pallas_call(
        functools.partial(local_kernel, factor, rows),
        grid=(kv_heads,),
        in_specs=[pl.BlockSpec((2, 1, tokens, head_dim), lambda g: (0, g, 0, 0))]
        + query_specs
        + [pl.BlockSpec((1, cols), lambda g: (0, 0)), pl.BlockSpec((tokens, 1), lambda g: (0, 0))],
        out_specs=[
            pl.BlockSpec((2, 1, tokens, head_dim), lambda g: (0, g, 0, 0)),
            pl.BlockSpec((tokens, grouped, head_dim), row_spec),
        ],
        out_shape=[
            jax.ShapeDtypeStruct((2, kv_heads, tokens, head_dim), jnp.float32),
            jax.ShapeDtypeStruct((tokens, heads, head_dim), jnp.float32),
        ],
        compiler_params=params,
        cost_estimate=pl.CostEstimate(flops=5 * work, bytes_accessed=2 * moved, transcendentals=0),
        name="local_block",
    )(kv, queries, grad_out, norm, term, docs, doc_col)

    far_specs = [
        pl.BlockSpec((1, 2, 1, tokens, head_dim), lambda g, idx: (idx[0], 0, g, 0, 0)),
        pl.BlockSpec((1, 2, 1, tokens, head_dim), lambda g, idx: (idx[1], 0, g, 0, 0)),
    ]
    far_kv = pl.pallas_call(
        functools.partial(listed_kernel, factor, rows),
        grid_spec=pltpu.PrefetchScalarGridSpec(
            num_scalar_prefetch=1,
            grid=(kv_heads,),
            in_specs=far_specs + query_specs,
            out_specs=pl.BlockSpec((2, 2, 1, tokens, head_dim), lambda g, idx: (0, 0, g, 0, 0)),
        ),
        out_shape=jax.ShapeDtypeStruct((2, 2, kv_heads, tokens, head_dim), jnp.bfloat16),
        compiler_params=params,
        cost_estimate=pl.CostEstimate(flops=8 * work, bytes_accessed=moved, transcendentals=0),
        name="listed_keys",
    )(index, gathered, gathered, queries, grad_out, norm, term)

    grad_queries = pl.pallas_call(
        functools.partial(query_kernel, factor, rows),
        grid_spec=pltpu.PrefetchScalarGridSpec(
            num_scalar_prefetch=1,
            grid=(kv_heads,),
            in_specs=far_specs + query_specs + [pl.BlockSpec((tokens, grouped, head_dim), row_spec)],
            out_specs=pl.BlockSpec((tokens, grouped, head_dim), row_spec),
        ),
        out_shape=jax.ShapeDtypeStruct((tokens, heads, head_dim), jnp.float32),
        compiler_params=params,
        cost_estimate=pl.CostEstimate(flops=6 * work, bytes_accessed=3 * moved, transcendentals=0),
        name="listed_queries",
    )(index, gathered, gathered, queries, grad_out, norm, term, near_query)

    swap = [(i, i ^ 1) for i in range(subs)]
    other_kv = lax.ppermute(far_kv, "sub", swap)
    other_index = lax.dynamic_index_in_dim(pairs, ctx * subs + (1 - sub), 0, keepdims=False)
    near = near_kv
    blocks = []
    for shift in range(ring):
        owner = lax.rem(ctx + shift, ring) * subs + sub
        block = jnp.zeros(kv.shape, jnp.float32)
        for which in range(2):
            block += jnp.where(index[which] == owner, far_kv[which].astype(jnp.float32), 0.0)
            block += jnp.where(other_index[which] == owner, other_kv[which].astype(jnp.float32), 0.0)
        blocks.append(block)
    near = near + blocks[0]
    for shift in range(1, ring):
        near = near + lax.ppermute(
            blocks[shift].astype(jnp.bfloat16), "ctx", [(i, (i + shift) % ring) for i in range(ring)]
        ).astype(jnp.float32)
    near = near.transpose(0, 2, 1, 3)
    return (grad_queries, near[0], near[1])


def solution(mesh):
    return jax.shard_map(
        body,
        mesh=mesh,
        in_specs=(
            P(("groups", "ctx", "sub"), "head", None),
            P(("groups", "ctx", "sub"), "head", None),
            P(("groups", "ctx", "sub"), "head", None),
            P(("groups", "ctx", "sub"), "head", None),
            P(("groups", "ctx", "sub"), "head"),
            P(("groups", "ctx", "sub"), "head"),
            P(("groups", "ctx", "sub")),
            P("groups", None),
        ),
        out_specs=(
            P(("groups", "ctx", "sub"), "head", None),
            P(("groups", "ctx", "sub"), "head", None),
            P(("groups", "ctx", "sub"), "head", None),
        ),
        check_vma=False,
    )
```

time: 79.9 us -> 84.6 us (1.059)
  between operations: 1.07 us -> 24.4 us
  matrix products: 14.8 us -> 0 us
  starting transfers between devices: 17 us -> 4.48 us
  Pallas kernels: 0 us -> 11.5 us
  local copies, waits for them, and re-layouts: 18.5 us -> 16.1 us
  waiting for transfers between devices: 24.7 us -> 23.4 us
    all_to_all x4 -> x0, waiting for transfers between devices: 24.7 us -> none  [the longest x1 10.5 us: body(): lax.all_to_all(outgoing, ('ctx', 'sub'), split_axis=1, concat_axis=1, til...]
    all_gather x0 -> x1, waiting for transfers between devices: none -> 23.4 us  [body(): gathered = lax.all_gather(kv, ('ctx', 'sub'), axis=0, tiled=False)]
    all_to_all x4 -> x0, starting transfers between devices: 17 us -> none  [the longest x1 6.33 us: body(): lax.all_to_all(stacked.reshape(spans, stripe, features), ('ctx', 'sub'),...]
    dot_general x16 -> x0, matrix products: 14.8 us -> none  [the longest x3 5.67 us: block_terms(): jnp.einsum('tghk,kgd->tghd', scores_low, key_blk, preferred_element_type=...]
    pallas_call x0 -> x3, Pallas kernels: none -> 11.5 us  [the longest x1 5.3 us: body(): pl.pallas_call(functools.partial(query_kernel, factor, rows), grid_spec=p...]
    ppermute x0 -> x4, starting transfers between devices: none -> 4.44 us  [the longest x3 4.14 us: body(): lax.ppermute(blocks[shift].astype(jnp.bfloat16), 'ctx', [(i, (i + shift)...]
    convert_element_type x0 -> x2, other arithmetic: none -> 2.22 us  [body(): blocks[shift].astype(jnp.bfloat16)]
    transpose x0 -> x2, other arithmetic: none -> 1.81 us  [the longest x1 1.14 us: body(): near = near.transpose(0, 2, 1, 3)]
  transfers between devices with their start and end apart: 4 -> 5, of which waited for: 4 -> 1; matrix products, arithmetic and copies ran while one was open for 19% -> 11% of each run, Pallas kernels for 0% -> 10%
where the time goes in v1:
time: 84.6 us; the launch traced here: 83.8 us
  between operations  24.4 us (29%)
  waiting for transfers between devices  23.4 us (28%)
  local copies, waits for them, and re-layouts  16.1 us (19%)
  Pallas kernels  11.5 us (14%)
  starting transfers between devices  4.48 us (5%)
  other arithmetic  4.03 us (5%)
    all_gather x1, waiting for transfers between devices, body(): gathered = lax.all_gather(kv, ('ctx', 'sub'), axis=0, tiled=False)  23.4 us
    unnamed x28, local copies, waits for them, and re-layouts  7.46 us
    pallas_call x1, Pallas kernels, body(): pl.pallas_call(functools.partial(query_kernel, factor, rows), grid_spec=p...  5.3 us
    ppermute x3, starting transfers between devices, body(): lax.ppermute(blocks[shift].astype(jnp.bfloat16), 'ctx', [(i, (i + shift)...  4.14 us
    pallas_call x1, Pallas kernels, body(): pl.pallas_call(functools.partial(listed_kernel, factor, rows), grid_spec=...  3.33 us
    pallas_call x1, Pallas kernels, body(): pl.pallas_call(functools.partial(local_kernel, factor, rows), grid=(kv_he...  2.88 us
    convert_element_type x2, other arithmetic, body(): blocks[shift].astype(jnp.bfloat16)  2.22 us
  transfers between devices with their start and end apart: 5, of which 1 were waited for; matrix products, arithmetic and copies ran while one was open for 11% of the time, Pallas kernels for 10%

profile of v1, /device:TPU:0, one launch (start us, length us, event | category | flops | bytes accessed | tf_op | source)
XLA Modules:
  0.0 83.8 jit_solution(4936410626074383442)
XLA Ops:
  7.2 0.0 all-gather.3.cloned.1.call-start
  7.2 0.9 %copy_bitcast_fusion = (bf16[1,128,2,128]{3,1,2,0:T(8,128)(2,1)S(1)}, bf16[1,128,2,128]{3,1,2,0:T(8,128)(2,1)S(1)}) fusion(bf16[128,2,128]{2,1,0:T(2,128)(2,1)} %param.10, bf16[128,2,128]{2,1,0:T(2,128)(2,1)} %param.9), kind=kLoop, calls=%fused_computation.43 | loop fusion | bytes 262144 | tf_op jit(solution)/shard_map/stack | solution.py:112
  8.1 0.7 maximum_bitcast_fusion.kv_ref
  8.8 0.0 all-gather.3.cloned.1.call-update
  8.8 0.8 copy.33
  9.6 0.1 reshape.102.norm_ref
  9.7 0.8 copy.34
  10.6 0.1 reshape.103.term_ref
  10.7 0.0 copy-start.7
  10.7 0.9 %fusion.24 = (s32[2]{0:T(128)S(1)}, s32[1,2]{0,1:T(2,128)S(1)}, s32[1,2]{0,1:T(2,128)S(1)}) fusion(s32[8,2]{0,1:T(2,128)} %param.15, s32[]{:T(128)S(6)} %select_n.129, s32[]{:T(128)S(6)} %select_n.132), kind=kLoop, calls=%fused_computation.47 | loop fusion | bytes 48 | tf_op jit(solution)/shard_map/jit(dynamic_index_in_dim)/dynamic_slice | solution.py:119
  11.6 0.0 copy-start.11
  11.6 23.4 %all-gather.3.cloned.1.call-done = bf16[16,2,128,128]{3,2,1,0:T(8,128)(2,1)} async-done(((bf16[2,2,128,128]{3,2,1,0:T(8,128)(2,1)}), bf16[16,2,128,128]{3,2,1,0:T(8,128)(2,1)}) %all-gather.3.cloned.1.call-update) | async-done | bytes 1048592 | tf_op jit(solution)/shard_map/all_gather | solution.py:118
  35.0 0.0 copy-start
  35.0 1.2 %copy-done = bf16[16,2,128,128]{3,2,1,0:T(8,128)(2,1)S(1)} copy-done((bf16[16,2,128,128]{3,2,1,0:T(8,128)(2,1)S(1)}, bf16[16,2,128,128]{3,2,1,0:T(8,128)(2,1)}, u32[]{:S(2)}) %copy-start) | copy-done | bytes 1048600
  36.2 0.0 copy-start.2
  36.2 1.2 %copy-done.2 = bf16[128,32,128]{2,1,0:T(8,128)(2,1)S(1)} copy-done((bf16[128,32,128]{2,1,0:T(8,128)(2,1)S(1)}, bf16[128,32,128]{2,1,0:T(8,128)(2,1)}, u32[]{:S(2)}) %copy-start.2) | copy-done | bytes 1048600
  37.5 1.2 %copy-done.4 = bf16[128,32,128]{2,1,0:T(8,128)(2,1)S(1)} copy-done((bf16[128,32,128]{2,1,0:T(8,128)(2,1)S(1)}, bf16[128,32,128]{2,1,0:T(8,128)(2,1)}, u32[]{:S(2)}) %copy-start.4) | copy-done | bytes 1048600
  38.7 3.3 %listed_keys.1 = bf16[2,2,2,128,128]{4,3,2,1,0:T(8,128)(2,1)S(1)} custom-call(s32[2]{0:T(128)S(1)} %get-tuple-element.16.index_ref, bf16[8,2,2,128,128]{4,3,2,1,0:T(8,128)(2,1)S(1)} %bitcast.40, bf16[8,2,2,128,128]{4,3,2,1,0:T(8,128)(2,1)S(1)} %bitcast.41, bf16[128,32,128]{2,1,0:T(8,128)(2,1)S(1)} %copy-done.2, bf16[128,32,128]{2,1,0:T(8,128)(2,1)S(1)} %copy-done.4, ...), custom_call_target="tpu_custom_call" | custom-call | flops 1073741824 | bytes 2097152 | tf_op jit(solution)/shard_map/listed_keys/pallas_call | solution.py:156
  42.0 0.0 copy-done.7
  42.0 0.0 copy-done.11
  42.0 0.3 collective-permute-start
  42.3 0.6 fusion.25
  45.4 0.0 copy-start.1
  53.1 1.4 %copy.37.doc_col_ref = s32[128,1]{1,0:T(8,128)} copy(s32[128,1]{0,1:T(1,128)} %bitcast.48) | data formatting | bytes 1024 | tf_op jit(solution)/shard_map/reshape | solution.py:116
  54.5 1.4 %broadcast_in_dim.22 = s32[128,16]{1,0:T(8,128)} broadcast(s32[128]{0:T(128)} %param.14), dimensions={0} | broadcast | bytes 8704 | tf_op jit(solution)/shard_map/broadcast_in_dim | solution.py:115
  55.9 1.5 %reshape_reshape.3.docs_ref = s32[1,2048]{1,0:T(1,128)} reshape(s32[128,16]{1,0:T(8,128)} %broadcast_in_dim.22) | data formatting | bytes 16384 | tf_op jit(solution)/shard_map/reshape;reshape | solution.py:115
  57.4 0.0 collective-permute-done
  57.4 1.1 %fusion.21 = bf16[2,2,128,128]{3,2,1,0:T(8,128)(2,1)S(1)} fusion(pred[]{:T(512)S(6)} %eq.63, pred[]{:T(512)S(6)} %eq.62, pred[]{:T(512)S(6)} %eq.61, pred[]{:T(512)S(6)} %eq.60, bf16[2,2,2,128,128]{4,3,2,1,0:T(8,128)(2,1)} %collective-permute-done, bf16[2,2,2,128,128]{4,3,2,1,0:T(8,128)(2,1)S(1)} %listed_keys.1), kind=kLoop, calls=%fused_computation.37 | loop fusion | flops 786432 | bytes 655364 | tf_op jit(solution)/shard_map/convert_element_type | solution.py:199
  58.5 2.0 %collective-permute-start.3 = (bf16[2,2,128,128]{3,2,1,0:T(8,128)(2,1)S(1)}, bf16[2,2,128,128]{3,2,1,0:T(8,128)(2,1)S(1)}, u32[]{:S(2)}, u32[]{:S(2)}) collective-permute-start(bf16[2,2,128,128]{3,2,1,0:T(8,128)(2,1)S(1)} %fusion.21), channel_id=1, source_target_pairs={{0,12},{4,0},{8,4},{12,8},{1,13},{5,1},{9,5},{13,9},{2,14},{6,2},{... | collective-permute-start | bytes 393224 | tf_op jit(solution)/shard_map/ppermute | solution.py:198
  60.5 1.1 %fusion.23 = (bf16[2,2,128,128]{3,2,1,0:T(8,128)(2,1)S(1)}, bf16[2,2,128,128]{3,2,1,0:T(8,128)(2,1)S(1)}) fusion(pred[]{:T(512)S(6)} %eq.55, pred[]{:T(512)S(6)} %eq.54, pred[]{:T(512)S(6)} %eq.53, pred[]{:T(512)S(6)} %eq.52, bf16[2,2,2,128,128]{4,3,2,1,0:T(8,128)(2,1)} %collective-permute-done, bf16[2,2,2,128,128]{4,3,2,1,0:T(8,128)(2,1)S(1)} %listed_keys.1, ...), kind=kLoop, calls=%fused_computation.39 | loop fusion | flops 1310720 | bytes 786440 | tf_op jit(solution)/shard_map/convert_element_type | solution.py:199
  61.7 0.1 collective-permute-start.1
  61.8 2.0 %collective-permute-start.2 = (bf16[2,2,128,128]{3,2,1,0:T(8,128)(2,1)S(1)}, bf16[2,2,128,128]{3,2,1,0:T(8,128)(2,1)S(1)}, u32[]{:S(2)}, u32[]{:S(2)}) collective-permute-start(bf16[2,2,128,128]{3,2,1,0:T(8,128)(2,1)S(1)} %get-tuple-element.19), channel_id=1, source_target_pairs={{0,8},{4,12},{8,0},{12,4},{1,9},{5,13},{9,1},{13,5},{2,10},{6,14},... | collective-permute-start | bytes 393224 | tf_op jit(solution)/shard_map/ppermute | solution.py:198
  63.8 0.0 copy-done.3
  63.8 0.0 copy-done.5
  63.8 0.0 copy-done.6
  63.8 0.7 copy-done.8
  64.5 0.8 copy-done.9
  65.4 0.7 copy-done.10
  66.1 2.9 %local_block.1 = (f32[2,2,128,128]{3,2,1,0:T(8,128)S(1)}, f32[128,32,128]{2,1,0:T(8,128)S(1)}) custom-call(bf16[2,2,128,128]{3,2,1,0:T(8,128)(2,1)S(1)} %copy-done.6, bf16[128,32,128]{2,1,0:T(8,128)(2,1)S(1)} %copy-done.3, bf16[128,32,128]{2,1,0:T(8,128)(2,1)S(1)} %copy-done.5, f32[2,1,2048]{2,1,0:T(1,128)S(1)} %reshape.102.norm_ref, ...), custom_call_target="tpu_custom_call" | custom-call | flops 671088640 | bytes 4194304 | tf_op jit(solution)/shard_map/local_block/pallas_call | solution.py:133
  68.9 0.0 copy-done.1
  69.0 0.0 copy-done.12
  69.0 5.3 %listed_queries.1 = f32[128,32,128]{2,1,0:T(8,128)} custom-call(s32[2]{0:T(128)S(1)} %copy-done.12, bf16[8,2,2,128,128]{4,3,2,1,0:T(8,128)(2,1)S(1)} %bitcast.42, bf16[8,2,2,128,128]{4,3,2,1,0:T(8,128)(2,1)S(1)} %bitcast.43, bf16[128,32,128]{2,1,0:T(8,128)(2,1)S(1)} %copy-done.3, bf16[128,32,128]{2,1,0:T(8,128)(2,1)S(1)} %copy-done.5, ...), custom_call_target="tpu_custom_call" | custom-call | flops 805306368 | bytes 6291456 | tf_op jit(solution)/shard_map/listed_queries/pallas_call | solution.py:170
  74.3 0.0 collective-permute-done.3
  74.3 0.0 collective-permute-done.1
  74.3 0.0 collective-permute-done.2
  74.3 1.1 %fusion.8 = f32[2,128,2,128]{3,1,2,0:T(8,128)S(1)} fusion(f32[2,2,128,128]{3,2,1,0:T(8,128)S(1)} %get-tuple-element.6, bf16[2,2,128,128]{3,2,1,0:T(8,128)(2,1)S(1)} %collective-permute-done.3, bf16[2,2,128,128]{3,2,1,0:T(8,128)(2,1)S(1)} %collective-permute-done.2, bf16[2,2,128,128]{3,2,1,0:T(8,128)(2,1)S(1)} %collective-permute-done.1, pred[]{:T(512)S(6)} %eq.51, ...), kind=kLoop, calls=%fused_computation.24 | loop fusion | flops 1179648 | bytes 1441796 | tf_op jit(solution)/shard_map/transpose | solution.py:201
  75.4 0.8 copy.43
  76.2 0.8 copy.42
  (9 shorter events, 0.0 us)
Async XLA Ops:
  7.2 27.8 %all-gather.3.cloned.1.call-start = ((), (), s32[]{:S(2)}) async-start(), calls=%async_computation | async-start | bytes 1179648 | tf_op jit(solution)/shard_map/all_gather | solution.py:118
  10.7 31.3 %copy-start.7 = (f32[2,1,2048]{2,1,0:T(1,128)}, f32[2,1,2048]{2,1,0:T(1,128)S(1)}, u32[]{:S(2)}) copy-start(f32[2,1,2048]{2,1,0:T(1,128)S(1)} %reshape.103.term_ref) | copy-start | bytes 49156
  11.6 30.4 %copy-start.11 = (s32[2]{0:T(128)}, s32[2]{0:T(128)S(1)}, u32[]{:S(2)}) copy-start(s32[2]{0:T(128)S(1)} %get-tuple-element.16.index_ref) | copy-start | bytes 28
  35.0 1.2 %copy-start = (bf16[16,2,128,128]{3,2,1,0:T(8,128)(2,1)S(1)}, bf16[16,2,128,128]{3,2,1,0:T(8,128)(2,1)}, u32[]{:S(2)}) copy-start(bf16[16,2,128,128]{3,2,1,0:T(8,128)(2,1)} %all-gather.3.cloned.1.call-done) | copy-start | bytes 3145732
  36.2 1.2 %copy-start.2 = (bf16[128,32,128]{2,1,0:T(8,128)(2,1)S(1)}, bf16[128,32,128]{2,1,0:T(8,128)(2,1)}, u32[]{:S(2)}) copy-start(bf16[128,32,128]{2,1,0:T(8,128)(2,1)} %query_ref.5) | copy-start | bytes 3145732
  37.5 1.2 %copy-start.4 = (bf16[128,32,128]{2,1,0:T(8,128)(2,1)S(1)}, bf16[128,32,128]{2,1,0:T(8,128)(2,1)}, u32[]{:S(2)}) copy-start(bf16[128,32,128]{2,1,0:T(8,128)(2,1)} %up_ref.5) | copy-start | bytes 3145732
  38.7 25.1 %copy-start.3 = (bf16[128,32,128]{2,1,0:T(8,128)(2,1)S(1)}, bf16[128,32,128]{2,1,0:T(8,128)(2,1)}, u32[]{:S(2)}) copy-start(bf16[128,32,128]{2,1,0:T(8,128)(2,1)} %query_ref.5) | copy-start | bytes 3145732
  38.7 25.1 %copy-start.5 = (bf16[128,32,128]{2,1,0:T(8,128)(2,1)S(1)}, bf16[128,32,128]{2,1,0:T(8,128)(2,1)}, u32[]{:S(2)}) copy-start(bf16[128,32,128]{2,1,0:T(8,128)(2,1)} %up_ref.5) | copy-start | bytes 3145732
  38.7 25.1 %copy-start.6 = (bf16[2,2,128,128]{3,2,1,0:T(8,128)(2,1)S(1)}, bf16[2,2,128,128]{3,2,1,0:T(8,128)(2,1)}, u32[]{:S(2)}) copy-start(bf16[2,2,128,128]{3,2,1,0:T(8,128)(2,1)} %maximum_bitcast_fusion.kv_ref) | copy-start | bytes 393220
  42.0 15.4 %collective-permute-start = (bf16[2,2,2,128,128]{4,3,2,1,0:T(8,128)(2,1)S(1)}, bf16[2,2,2,128,128]{4,3,2,1,0:T(8,128)(2,1)}, u32[]{:S(2)}, u32[]{:S(2)}) collective-permute-start(bf16[2,2,2,128,128]{4,3,2,1,0:T(8,128)(2,1)S(1)} %listed_keys.1), channel_id=1, source_target_pairs={{0,1},{1,0},{2,3},{3,2},{4,5},{5,4},{6,7},{7,6},{8,9},{9,8},{10,11... | collective-permute-start | bytes 786440 | tf_op jit(solution)/shard_map/ppermute | solution.py:185
  45.4 23.5 %copy-start.1 = (bf16[16,2,128,128]{3,2,1,0:T(8,128)(2,1)S(1)}, bf16[16,2,128,128]{3,2,1,0:T(8,128)(2,1)}, u32[]{:S(2)}) copy-start(bf16[16,2,128,128]{3,2,1,0:T(8,128)(2,1)} %all-gather.3.cloned.1.call-done) | copy-start | bytes 3145732
  57.4 11.5 %copy-start.12 = (s32[2]{0:T(128)S(1)}, s32[2]{0:T(128)}, u32[]{:S(2)}) copy-start(s32[2]{0:T(128)} %copy-done.11) | copy-start | bytes 28
  58.5 15.8 %collective-permute-start.3 = (bf16[2,2,128,128]{3,2,1,0:T(8,128)(2,1)S(1)}, bf16[2,2,128,128]{3,2,1,0:T(8,128)(2,1)S(1)}, u32[]{:S(2)}, u32[]{:S(2)}) collective-permute-start(bf16[2,2,128,128]{3,2,1,0:T(8,128)(2,1)S(1)} %fusion.21), channel_id=1, source_target_pairs={{0,12},{4,0},{8,4},{12,8},{1,13},{5,1},{9,5},{13,9},{2,14},{6,2},{... | collective-permute-start | bytes 393224 | tf_op jit(solution)/shard_map/ppermute | solution.py:198
  61.7 12.6 %collective-permute-start.1 = (bf16[2,2,128,128]{3,2,1,0:T(8,128)(2,1)S(1)}, bf16[2,2,128,128]{3,2,1,0:T(8,128)(2,1)S(1)}, u32[]{:S(2)}, u32[]{:S(2)}) collective-permute-start(bf16[2,2,128,128]{3,2,1,0:T(8,128)(2,1)S(1)} %get-tuple-element.18), channel_id=1, source_target_pairs={{0,4},{4,8},{8,12},{12,0},{1,5},{5,9},{9,13},{13,1},{2,6},{6,10},{... | collective-permute-start | bytes 393224 | tf_op jit(solution)/shard_map/ppermute | solution.py:198
  61.8 12.5 %collective-permute-start.2 = (bf16[2,2,128,128]{3,2,1,0:T(8,128)(2,1)S(1)}, bf16[2,2,128,128]{3,2,1,0:T(8,128)(2,1)S(1)}, u32[]{:S(2)}, u32[]{:S(2)}) collective-permute-start(bf16[2,2,128,128]{3,2,1,0:T(8,128)(2,1)S(1)} %get-tuple-element.19), channel_id=1, source_target_pairs={{0,8},{4,12},{8,0},{12,4},{1,9},{5,13},{9,1},{13,5},{2,10},{6,14},... | collective-permute-start | bytes 393224 | tf_op jit(solution)/shard_map/ppermute | solution.py:198
  63.8 0.7 copy-start.8
  64.5 0.8 %copy-start.9 = (s32[128,1]{1,0:T(8,128)S(1)}, s32[128,1]{1,0:T(8,128)}, u32[]{:S(2)}) copy-start(s32[128,1]{1,0:T(8,128)} %copy.37.doc_col_ref) | copy-start | bytes 1540
  65.4 0.7 copy-start.10
Sparse Core Ops, SparseCore 0:
  10.2 24.7 all-gather.2

commit v2 on v1

v2 whole, which is shorter than its diff:
```python
import functools

import jax
import jax.numpy as jnp
from jax import lax
from jax.experimental import pallas as pl
from jax.experimental.pallas import tpu as pltpu
from jax.sharding import PartitionSpec as P

QH = 64
KVH = 4
LOG2E = 1.4426950408889634
ROWS = 512
VMEM_LIMIT = 24 * 1024 * 1024

VMEM_SPEC = pl.BlockSpec(memory_space=pltpu.VMEM)
SMEM_SPEC = pl.BlockSpec(memory_space=pltpu.SMEM)
ANY_SPEC = pl.BlockSpec(memory_space=pl.ANY)


def rows_dot(left, right):
    return lax.dot_general(left, right, (((1,), (1,)), ((), ())), preferred_element_type=jnp.float32)


def tile_terms(key_blk, value_blk, query_blk, upstream, log_norm, row_terms, allowed, factor):
    scores = rows_dot(key_blk, query_blk)
    probs = jnp.exp2(scores * (factor * LOG2E) - log_norm * LOG2E)
    if allowed is not None:
        probs = jnp.where(allowed, probs, 0.0)
    grad_probs = rows_dot(value_blk, upstream)
    grad_scores = probs * (grad_probs - row_terms)
    return probs.astype(jnp.bfloat16), grad_scores.astype(jnp.bfloat16)


def chunks(query_ref, rows):
    tokens, grouped, head_dim = query_ref.shape
    step = rows // grouped
    return [(i, slice(i * step, (i + 1) * step), slice(i * rows, (i + 1) * rows)) for i in range(tokens // step)]


def pack_kernel(key_ref, value_ref, kv_ref):
    for head in range(key_ref.shape[1]):
        kv_ref[0, head] = key_ref[:, head, :]
        kv_ref[1, head] = value_ref[:, head, :]


def choose_kernel(subs, place_ref, pairs_ref, *refs):
    *column, near_ref, out_ref = refs
    ring = len(column)
    ctx, sub = place_ref[0], place_ref[1]
    for which in range(2):
        span = pairs_ref[which, ctx * subs + (1 - sub)]
        shift = lax.rem(ctx - span // subs + ring, ring)
        for step in range(ring):
            @pl.when(shift == step)
            def _():
                out_ref[which] = column[step][...]


def far_blocks(subs, place_ref, pairs_ref, column, other_ref, far_ref):
    ring = len(column)
    ctx, sub = place_ref[0], place_ref[1]
    for which in range(2):
        span = pairs_ref[which, ctx * subs + sub]
        shift = lax.rem(ctx - span // subs + ring, ring)
        mine = lax.rem(span, subs) == sub

        @pl.when(jnp.logical_not(mine))
        def _():
            far_ref[which] = other_ref[which]

        for step in range(ring):
            @pl.when(mine & (shift == step))
            def _():
                far_ref[which] = column[step][...]


def local_kernel(factor, rows, kv_ref, query_ref, up_ref, norm_ref, term_ref, docs_ref, doc_col_ref,
                 dkv_ref, dq_ref):
    tokens, grouped, head_dim = query_ref.shape
    key_blk, value_blk = kv_ref[0, 0], kv_ref[1, 0]
    grad_key = jnp.zeros((tokens, head_dim), jnp.float32)
    grad_val = jnp.zeros((tokens, head_dim), jnp.float32)
    for i, toks, cols in chunks(query_ref, rows):
        query_blk = query_ref[toks].reshape(rows, head_dim)
        upstream = up_ref[toks].reshape(rows, head_dim)
        position = lax.broadcasted_iota(jnp.int32, (tokens, rows), 1) // grouped + toks.start
        allowed = (lax.broadcasted_iota(jnp.int32, (tokens, rows), 0) <= position) & (
            doc_col_ref[...] == docs_ref[:, cols]
        )
        probs, grads = tile_terms(
            key_blk, value_blk, query_blk, upstream, norm_ref[0, :, cols], term_ref[0, :, cols], allowed, factor
        )
        grad_val += jnp.dot(probs, upstream, preferred_element_type=jnp.float32)
        grad_key += jnp.dot(grads, query_blk, preferred_element_type=jnp.float32)
        grad_query = lax.dot_general(
            grads, key_blk, (((0,), (0,)), ((), ())), preferred_element_type=jnp.float32
        )
        dq_ref[toks] = (grad_query * factor).reshape(rows // grouped, grouped, head_dim)
    dkv_ref[0, 0] = grad_key * factor
    dkv_ref[1, 0] = grad_val


def listed_kernel(factor, rows, subs, place_ref, pairs_ref, *refs):
    (*column, other_ref, query_ref, up_ref, norm_ref, term_ref, dkv_ref, far_ref) = refs
    tokens, grouped, head_dim = query_ref.shape
    head = pl.program_id(0)

    @pl.when(head == 0)
    def _():
        far_blocks(subs, place_ref, pairs_ref, column, other_ref, far_ref)

    key_blk = jnp.concatenate([far_ref[0, 0, head], far_ref[1, 0, head]], axis=0)
    value_blk = jnp.concatenate([far_ref[0, 1, head], far_ref[1, 1, head]], axis=0)
    grad_key = jnp.zeros((2 * tokens, head_dim), jnp.float32)
    grad_val = jnp.zeros((2 * tokens, head_dim), jnp.float32)
    for i, toks, cols in chunks(query_ref, rows):
        query_blk = query_ref[toks].reshape(rows, head_dim)
        upstream = up_ref[toks].reshape(rows, head_dim)
        probs, grads = tile_terms(
            key_blk, value_blk, query_blk, upstream, norm_ref[0, :, cols], term_ref[0, :, cols], None, factor
        )
        grad_val += jnp.dot(probs, upstream, preferred_element_type=jnp.float32)
        grad_key += jnp.dot(grads, query_blk, preferred_element_type=jnp.float32)
    grad_key = (grad_key * factor).astype(dkv_ref.dtype)
    grad_val = grad_val.astype(dkv_ref.dtype)
    for which in range(2):
        dkv_ref[which, 0, 0] = grad_key[which * tokens:(which + 1) * tokens]
        dkv_ref[which, 1, 0] = grad_val[which * tokens:(which + 1) * tokens]


def query_kernel(factor, rows, subs, place_ref, pairs_ref, *refs):
    (*column, other_ref, query_ref, up_ref, norm_ref, term_ref, near_ref, dq_ref, far_ref) = refs
    tokens, grouped, head_dim = query_ref.shape
    head = pl.program_id(0)

    @pl.when(head == 0)
    def _():
        far_blocks(subs, place_ref, pairs_ref, column, other_ref, far_ref)

    key_blk = jnp.concatenate([far_ref[0, 0, head], far_ref[1, 0, head]], axis=0)
    value_blk = jnp.concatenate([far_ref[0, 1, head], far_ref[1, 1, head]], axis=0)
    for i, toks, cols in chunks(query_ref, rows):
        query_blk = query_ref[toks].reshape(rows, head_dim)
        upstream = up_ref[toks].reshape(rows, head_dim)
        probs, grads = tile_terms(
            key_blk, value_blk, query_blk, upstream, norm_ref[0, :, cols], term_ref[0, :, cols], None, factor
        )
        grad_query = lax.dot_general(
            grads, key_blk, (((0,), (0,)), ((), ())), preferred_element_type=jnp.float32
        )
        dq_ref[toks] = near_ref[toks] + (grad_query * factor).reshape(rows // grouped, grouped, head_dim)


def combine_kernel(subs, place_ref, pairs_ref, mine_ref, other_ref, *out_refs):
    ring = len(out_refs)
    ctx, sub = place_ref[0], place_ref[1]
    parts = []
    for ref, core in ((mine_ref, sub), (other_ref, 1 - sub)):
        for which in range(2):
            span = pairs_ref[which, ctx * subs + core]
            shift = lax.rem(span // subs - ctx + ring, ring)
            parts.append((ref, which, jnp.where(lax.rem(span, subs) == sub, shift, ring)))
    for step, out_ref in enumerate(out_refs):
        total = jnp.zeros(out_ref.shape, jnp.float32)
        for ref, which, shift in parts:
            total += jnp.where(shift == step, ref[which].astype(jnp.float32), 0.0)
        out_ref[...] = total.astype(out_ref.dtype)


def total_kernel(near_ref, own_ref, *refs):
    *column, dk_ref, dv_ref = refs
    for part, out_ref in enumerate((dk_ref, dv_ref)):
        for head in range(out_ref.shape[1]):
            total = near_ref[part, head] + own_ref[part, head]
            for ref in column:
                total += ref[part, head].astype(jnp.float32)
            out_ref[:, head, :] = total


def body(queries, keys, values, grad_out, row_lse, row_delta, doc_ids, pairs):
    tokens, heads, head_dim = queries.shape
    kv_heads = keys.shape[1]
    grouped = QH // KVH
    factor = head_dim ** (-0.5)
    ring = lax.axis_size("ctx")
    subs = lax.axis_size("sub")
    rows = min(ROWS, tokens * grouped)
    cols = tokens * grouped
    place = jnp.stack([lax.axis_index("ctx"), lax.axis_index("sub")])
    listed = pairs.T
    span_shape = (2, kv_heads, tokens, head_dim)

    def shifted(array, shift):
        return lax.ppermute(array, "ctx", [(i, (i + shift) % ring) for i in range(ring)])

    def swapped(array):
        return lax.ppermute(array, "sub", [(i, i ^ 1) for i in range(subs)])

    small = pltpu.CompilerParams(vmem_limit_bytes=VMEM_LIMIT)
    kv = pl.pallas_call(
        pack_kernel,
        in_specs=[VMEM_SPEC] * 2,
        out_specs=VMEM_SPEC,
        out_shape=jax.ShapeDtypeStruct(span_shape, jnp.bfloat16),
        compiler_params=small,
        name="pack",
    )(keys, values)
    column = [kv] + [shifted(kv, shift) for shift in range(1, ring)]

    norm = row_lse.reshape(tokens, kv_heads, grouped).transpose(1, 0, 2).reshape(kv_heads, 1, cols)
    term = row_delta.reshape(tokens, kv_heads, grouped).transpose(1, 0, 2).reshape(kv_heads, 1, cols)
    docs = jnp.repeat(doc_ids, grouped).reshape(1, cols)
    doc_col = doc_ids.reshape(tokens, 1)

    params = pltpu.CompilerParams(vmem_limit_bytes=VMEM_LIMIT, dimension_semantics=("arbitrary",))
    row_spec = pl.BlockSpec((tokens, grouped, head_dim), lambda g: (0, g, 0))
    lane_spec = pl.BlockSpec((1, 1, cols), lambda g: (g, 0, 0))
    query_specs = [row_spec, row_spec, lane_spec, lane_spec]
    work = 2 * tokens * tokens * heads * head_dim
    moved = 2 * queries.size * 2

    near_kv, near_query = pl.pallas_call(
        functools.partial(local_kernel, factor, rows),
        grid=(kv_heads,),
        in_specs=[pl.BlockSpec((2, 1, tokens, head_dim), lambda g: (0, g, 0, 0))]
        + query_specs
        + [pl.BlockSpec((1, cols), lambda g: (0, 0)), pl.BlockSpec((tokens, 1), lambda g: (0, 0))],
        out_specs=[pl.BlockSpec((2, 1, tokens, head_dim), lambda g: (0, g, 0, 0)), row_spec],
        out_shape=[
            jax.ShapeDtypeStruct(span_shape, jnp.float32),
            jax.ShapeDtypeStruct((tokens, heads, head_dim), jnp.float32),
        ],
        compiler_params=params,
        cost_estimate=pl.CostEstimate(flops=5 * work, bytes_accessed=2 * moved, transcendentals=0),
        name="local_block",
    )(kv, queries, grad_out, norm, term, docs, doc_col)

    chosen = pl.pallas_call(
        functools.partial(choose_kernel, subs),
        in_specs=[SMEM_SPEC] * 2 + [VMEM_SPEC] * ring + [ANY_SPEC],
        out_specs=VMEM_SPEC,
        out_shape=jax.ShapeDtypeStruct((2, *span_shape), jnp.bfloat16),
        compiler_params=small,
        name="choose",
    )(place, listed, *column, near_kv)
    other = swapped(chosen)

    far_specs = (
        [SMEM_SPEC] * 2
        + [pl.BlockSpec(span_shape, lambda g: (0, 0, 0, 0))] * ring
        + [pl.BlockSpec((2, *span_shape), lambda g: (0, 0, 0, 0, 0))]
        + query_specs
    )
    far_scratch = [pltpu.VMEM((2, *span_shape), jnp.bfloat16)]
    far_args = (place, listed, *column, other, queries, grad_out, norm, term)
    far_kv = pl.pallas_call(
        functools.partial(listed_kernel, factor, rows, subs),
        grid=(kv_heads,),
        in_specs=far_specs,
        out_specs=pl.BlockSpec((2, 2, 1, tokens, head_dim), lambda g: (0, 0, g, 0, 0)),
        out_shape=jax.ShapeDtypeStruct((2, *span_shape), jnp.bfloat16),
        scratch_shapes=far_scratch,
        compiler_params=params,
        cost_estimate=pl.CostEstimate(flops=8 * work, bytes_accessed=moved, transcendentals=0),
        name="listed_keys",
    )(*far_args)
    other_kv = swapped(far_kv)

    blocks = pl.pallas_call(
        functools.partial(combine_kernel, subs),
        in_specs=[SMEM_SPEC] * 2 + [VMEM_SPEC] * 2,
        out_specs=[VMEM_SPEC] * ring,
        out_shape=[jax.ShapeDtypeStruct(span_shape, jnp.float32)]
        + [jax.ShapeDtypeStruct(span_shape, jnp.bfloat16)] * (ring - 1),
        compiler_params=small,
        name="combine",
    )(place, listed, far_kv, other_kv)
    arrived = [shifted(blocks[shift], shift) for shift in range(1, ring)]

    grad_queries = pl.pallas_call(
        functools.partial(query_kernel, factor, rows, subs),
        grid=(kv_heads,),
        in_specs=far_specs + [row_spec],
        out_specs=row_spec,
        out_shape=jax.ShapeDtypeStruct((tokens, heads, head_dim), jnp.float32),
        scratch_shapes=far_scratch,
        compiler_params=params,
        cost_estimate=pl.CostEstimate(flops=6 * work, bytes_accessed=3 * moved, transcendentals=0),
        name="listed_queries",
    )(*far_args, near_query)

    grad_keys, grad_values = pl.pallas_call(
        total_kernel,
        in_specs=[VMEM_SPEC] * (ring + 1),
        out_specs=[VMEM_SPEC] * 2,
        out_shape=[jax.ShapeDtypeStruct((tokens, kv_heads, head_dim), jnp.float32)] * 2,
        compiler_params=small,
        name="total",
    )(near_kv, blocks[0], *arrived)
    return (grad_queries, grad_keys, grad_values)


def solution(mesh):
    return jax.shard_map(
        body,
        mesh=mesh,
        in_specs=(
            P(("groups", "ctx", "sub"), "head", None),
            P(("groups", "ctx", "sub"), "head", None),
            P(("groups", "ctx", "sub"), "head", None),
            P(("groups", "ctx", "sub"), "head", None),
            P(("groups", "ctx", "sub"), "head"),
            P(("groups", "ctx", "sub"), "head"),
            P(("groups", "ctx", "sub")),
            P("groups", None),
        ),
        out_specs=(
            P(("groups", "ctx", "sub"), "head", None),
            P(("groups", "ctx", "sub"), "head", None),
            P(("groups", "ctx", "sub"), "head", None),
        ),
        check_vma=False,
    )
```

time: 84.6 us -> 49.4 us (0.58)
  the two profiles are of different devices: /device:TPU:0 before, /device:TPU:9 now
where the time goes in v2:
time: 49.4 us; the launch traced here: 48.7 us
  Pallas kernels  15.8 us (32%)
  local copies, waits for them, and re-layouts  15 us (30%)
  starting transfers between devices  8.87 us (18%)
  waiting for transfers between devices  8.23 us (17%)
  between operations  0.74 us (1%)
    unnamed x30, local copies, waits for them, and re-layouts  9.68 us
    ppermute x6, starting transfers between devices, shifted(): lax.ppermute(array, 'ctx', [(i, (i + shift) % ring) for i in range(ring)])  6.85 us
    ppermute x6, waiting for transfers between devices, shifted(): lax.ppermute(array, 'ctx', [(i, (i + shift) % ring) for i in range(ring)])  5.91 us
    pallas_call x1, Pallas kernels, body(): pl.pallas_call(functools.partial(query_kernel, factor, rows, subs), grid=...  5.74 us
    pallas_call x1, Pallas kernels, body(): pl.pallas_call(functools.partial(listed_kernel, factor, rows, subs), grid...  3.82 us
    pallas_call x1, Pallas kernels, body(): pl.pallas_call(functools.partial(local_kernel, factor, rows), grid=(kv_he...  2.87 us
    ppermute x2, waiting for transfers between devices, swapped(): return lax.ppermute(array, 'sub', [(i, i ^ 1) for i in range(subs)])  2.33 us
    ppermute x2, starting transfers between devices, swapped(): return lax.ppermute(array, 'sub', [(i, i ^ 1) for i in range(subs)])  2.01 us
  transfers between devices with their start and end apart: 8, of which 4 were waited for; matrix products, arithmetic and copies ran while one was open for 11% of the time, Pallas kernels for 18%

profile of v2, /device:TPU:9, one launch (start us, length us, event | category | flops | bytes accessed | tf_op | source)
XLA Modules:
  0.0 48.7 jit_solution(1287751448524795683)
XLA Ops:
  0.6 0.0 copy-start.9
  0.6 0.8 %copy-done.9 = bf16[128,2,128]{2,1,0:T(2,128)(2,1)S(1)} copy-done((bf16[128,2,128]{2,1,0:T(2,128)(2,1)S(1)}, bf16[128,2,128]{2,1,0:T(2,128)(2,1)}, u32[]{:S(2)}) %copy-start.9) | copy-done | bytes 65560
  1.5 0.8 %copy-done.10 = bf16[128,2,128]{2,1,0:T(2,128)(2,1)S(1)} copy-done((bf16[128,2,128]{2,1,0:T(2,128)(2,1)S(1)}, bf16[128,2,128]{2,1,0:T(2,128)(2,1)}, u32[]{:S(2)}) %copy-start.10) | copy-done | bytes 65560
  2.3 0.4 pack.1.kv_ref.refs_0_
  2.7 0.1 collective-permute-start.2
  2.7 2.5 %collective-permute-start.1 = (bf16[2,2,128,128]{3,2,1,0:T(8,128)(2,1)S(1)}, bf16[2,2,128,128]{3,2,1,0:T(8,128)(2,1)}, u32[]{:S(2)}, u32[]{:S(2)}) collective-permute-start(bf16[2,2,128,128]{3,2,1,0:T(8,128)(2,1)S(1)} %pack.1.kv_ref.refs_0_), channel_id=1, source_target_pairs={{0,8},{4,12},{8,0},{12,4},{1,9},{5,13},{9,1},{13,5},{2,10},{6,14},... | collective-permute-start | bytes 393224 | tf_op jit(solution)/shard_map/ppermute | solution.py:195
  5.2 2.2 %collective-permute-start = (bf16[2,2,128,128]{3,2,1,0:T(8,128)(2,1)S(1)}, bf16[2,2,128,128]{3,2,1,0:T(8,128)(2,1)}, u32[]{:S(2)}, u32[]{:S(2)}) collective-permute-start(bf16[2,2,128,128]{3,2,1,0:T(8,128)(2,1)S(1)} %pack.1.kv_ref.refs_0_), channel_id=1, source_target_pairs={{0,4},{4,8},{8,12},{12,0},{1,5},{5,9},{9,13},{13,1},{2,6},{6,10},{... | collective-permute-start | bytes 393224 | tf_op jit(solution)/shard_map/ppermute | solution.py:195
  7.4 1.4 %copy.18.doc_col_ref = s32[128,1]{1,0:T(8,128)} copy(s32[128,1]{0,1:T(1,128)} %bitcast.16) | data formatting | bytes 1024 | tf_op jit(solution)/shard_map/reshape | solution.py:214
  8.8 0.7 %broadcast_in_dim.3 = s32[128,16]{1,0:T(8,128)S(1)} broadcast(s32[128]{0:T(128)} %param.14), dimensions={0} | broadcast | bytes 8704 | tf_op jit(solution)/shard_map/broadcast_in_dim | solution.py:213
  9.5 0.7 %reshape_reshape.3.docs_ref = s32[1,2048]{1,0:T(1,128)} reshape(s32[128,16]{1,0:T(8,128)S(1)} %broadcast_in_dim.3) | data formatting | bytes 16384 | tf_op jit(solution)/shard_map/reshape;reshape | solution.py:213
  10.2 0.8 %copy.14 = f32[128,2,16]{2,0,1:T(8,128)S(1)} copy(f32[128,2,16]{0,2,1:T(8,128)} %bitcast.14) | data formatting | bytes 32768 | tf_op jit(solution)/shard_map/reshape | solution.py:211
  11.0 0.1 reshape.26.norm_ref.refs_7_
  11.2 0.8 %copy.15 = f32[128,2,16]{2,0,1:T(8,128)S(1)} copy(f32[128,2,16]{0,2,1:T(8,128)} %bitcast.15) | data formatting | bytes 32768 | tf_op jit(solution)/shard_map/reshape | solution.py:212
  12.0 0.7 %reshape.27.term_ref.refs_8_ = f32[2,1,2048]{2,1,0:T(1,128)} reshape(f32[2,128,16]{2,1,0:T(8,128)S(1)} %bitcast.13) | data formatting | bytes 32768 | tf_op jit(solution)/shard_map/reshape | solution.py:212
  12.7 1.2 %copy-done = bf16[128,32,128]{2,1,0:T(8,128)(2,1)S(1)} copy-done((bf16[128,32,128]{2,1,0:T(8,128)(2,1)S(1)}, bf16[128,32,128]{2,1,0:T(8,128)(2,1)}, u32[]{:S(2)}) %copy-start) | copy-done | bytes 1048600
  13.9 1.2 %copy-done.2 = bf16[128,32,128]{2,1,0:T(8,128)(2,1)S(1)} copy-done((bf16[128,32,128]{2,1,0:T(8,128)(2,1)S(1)}, bf16[128,32,128]{2,1,0:T(8,128)(2,1)}, u32[]{:S(2)}) %copy-start.2) | copy-done | bytes 1048600
  15.2 0.7 %copy-done.5 = f32[2,1,2048]{2,1,0:T(1,128)S(1)} copy-done((f32[2,1,2048]{2,1,0:T(1,128)S(1)}, f32[2,1,2048]{2,1,0:T(1,128)}, u32[]{:S(2)}) %copy-start.5) | copy-done | bytes 16408
  15.9 0.8 %copy-done.8 = s32[128,1]{1,0:T(8,128)S(1)} copy-done((s32[128,1]{1,0:T(8,128)S(1)}, s32[128,1]{1,0:T(8,128)}, u32[]{:S(2)}) %copy-start.8) | copy-done | bytes 536
  16.7 0.7 %copy-done.14 = s32[1,2048]{1,0:T(1,128)S(1)} copy-done((s32[1,2048]{1,0:T(1,128)S(1)}, s32[1,2048]{1,0:T(1,128)}, u32[]{:S(2)}) %copy-start.14) | copy-done | bytes 8216
  17.4 2.9 %local_block.1 = (f32[2,2,128,128]{3,2,1,0:T(8,128)S(1)}, f32[128,32,128]{2,1,0:T(8,128)S(1)}) custom-call(bf16[2,2,128,128]{3,2,1,0:T(8,128)(2,1)S(1)} %pack.1.kv_ref.refs_0_, bf16[128,32,128]{2,1,0:T(8,128)(2,1)S(1)} %copy-done, bf16[128,32,128]{2,1,0:T(8,128)(2,1)S(1)} %copy-done.2, f32[2,1,2048]{2,1,0:T(1,128)S(1)} %reshape.26.norm_ref.refs_7_, ...), custom_call_target="tpu_custom_call" | custom-call | flops 671088640 | bytes 4194304 | tf_op jit(solution)/shard_map/local_block/pallas_call | solution.py:223
  20.3 0.1 pad_add_fusion.place_ref
  20.4 0.0 collective-permute-done.2.refs_3_
  20.4 0.0 collective-permute-done.1.refs_2_
  20.4 0.0 collective-permute-done.refs_1_
  20.4 0.0 copy-start.11
  20.4 0.7 %copy-done.11 = s32[8,2]{0,1:T(2,128)S(1)} copy-done((s32[8,2]{0,1:T(2,128)S(1)}, s32[8,2]{0,1:T(2,128)}, u32[]{:S(2)}) %copy-start.11) | copy-done | bytes 88
  21.1 1.2 %choose.1 = bf16[2,2,2,128,128]{4,3,2,1,0:T(8,128)(2,1)S(1)} custom-call(s32[2]{0:T(128)S(1)} %pad_add_fusion.place_ref, s32[2,8]{1,0:T(2,128)S(1)} %bitcast.8, bf16[2,2,128,128]{3,2,1,0:T(8,128)(2,1)S(1)} %pack.1.kv_ref.refs_0_, bf16[2,2,128,128]{3,2,1,0:T(8,128)(2,1)} %collective-permute-done.refs_1_, ...), custom_call_target="tpu_custom_call" | custom-call | tf_op jit(solution)/shard_map/choose/pallas_call | solution.py:239
  22.3 1.6 %collective-permute-start.3 = (bf16[2,2,2,128,128]{4,3,2,1,0:T(8,128)(2,1)S(1)}, bf16[2,2,2,128,128]{4,3,2,1,0:T(8,128)(2,1)S(1)}, u32[]{:S(2)}, u32[]{:S(2)}) collective-permute-start(bf16[2,2,2,128,128]{4,3,2,1,0:T(8,128)(2,1)S(1)} %choose.1), channel_id=1, source_target_pairs={{0,1},{1,0},{2,3},{3,2},{4,5},{5,4},{6,7},{7,6},{8,9},{9,8},{10,11... | collective-permute-start | bytes 786440 | tf_op jit(solution)/shard_map/ppermute | solution.py:198
  23.9 1.2 %collective-permute-done.3.refs_4_ = bf16[2,2,2,128,128]{4,3,2,1,0:T(8,128)(2,1)S(1)} collective-permute-done((bf16[2,2,2,128,128]{4,3,2,1,0:T(8,128)(2,1)S(1)}, bf16[2,2,2,128,128]{4,3,2,1,0:T(8,128)(2,1)S(1)}, u32[]{:S(2)}, u32[]{:S(2)}) %collective-permute-start.3) | collective-permute-done | bytes 262176 | tf_op jit(solution)/shard_map/ppermute | solution.py:198
  25.0 0.0 copy-done.1
  25.0 1.2 %copy-done.3 = bf16[128,32,128]{2,1,0:T(8,128)(2,1)S(1)} copy-done((bf16[128,32,128]{2,1,0:T(8,128)(2,1)S(1)}, bf16[128,32,128]{2,1,0:T(8,128)(2,1)}, u32[]{:S(2)}) %copy-start.3) | copy-done | bytes 1048600
  26.3 0.7 %copy-done.6 = f32[2,1,2048]{2,1,0:T(1,128)S(1)} copy-done((f32[2,1,2048]{2,1,0:T(1,128)S(1)}, f32[2,1,2048]{2,1,0:T(1,128)}, u32[]{:S(2)}) %copy-start.6) | copy-done | bytes 16408
  27.0 0.7 %copy-done.12 = s32[8,2]{0,1:T(2,128)S(1)} copy-done((s32[8,2]{0,1:T(2,128)S(1)}, s32[8,2]{0,1:T(2,128)}, u32[]{:S(2)}) %copy-start.12) | copy-done | bytes 88
  27.7 3.8 %listed_keys.1.mine_ref = bf16[2,2,2,128,128]{4,3,2,1,0:T(8,128)(2,1)S(1)} custom-call(s32[2]{0:T(128)S(1)} %pad_add_fusion.place_ref, s32[2,8]{1,0:T(2,128)S(1)} %bitcast.9, bf16[2,2,128,128]{3,2,1,0:T(8,128)(2,1)S(1)} %pack.1.kv_ref.refs_0_, bf16[2,2,128,128]{3,2,1,0:T(8,128)(2,1)} %collective-permute-done.refs_1_, ...), custom_call_target="tpu_custom_call" | custom-call | flops 1073741824 | bytes 2097152 | tf_op jit(solution)/shard_map/listed_keys/pallas_call | solution.py:257
  31.5 0.4 collective-permute-start.4
  31.9 1.2 %collective-permute-done.4.other_ref = bf16[2,2,2,128,128]{4,3,2,1,0:T(8,128)(2,1)S(1)} collective-permute-done((bf16[2,2,2,128,128]{4,3,2,1,0:T(8,128)(2,1)S(1)}, bf16[2,2,2,128,128]{4,3,2,1,0:T(8,128)(2,1)S(1)}, u32[]{:S(2)}, u32[]{:S(2)}) %collective-permute-start.4) | collective-permute-done | bytes 262176 | tf_op jit(solution)/shard_map/ppermute | solution.py:198
  33.1 0.0 copy-done.13
  33.1 1.0 %combine.1 = (f32[2,2,128,128]{3,2,1,0:T(8,128)S(1)}, bf16[2,2,128,128]{3,2,1,0:T(8,128)(2,1)S(1)}, bf16[2,2,128,128]{3,2,1,0:T(8,128)(2,1)S(1)}, bf16[2,2,128,128]{3,2,1,0:T(8,128)(2,1)S(1)}) custom-call(s32[2]{0:T(128)S(1)} %pad_add_fusion.place_ref, s32[2,8]{1,0:T(2,128)S(1)} %bitcast.10, bf16[2,2,2,128,128]{4,3,2,1,0:T(8,128)(2,1)S(1)} %listed_keys.1.mine_ref, ...), custom_call_target="tpu_custom_call" | custom-call | tf_op jit(solution)/shard_map/combine/pallas_call | solution.py:270
  34.1 0.1 collective-permute-start.5
  34.1 1.3 %collective-permute-start.6 = (bf16[2,2,128,128]{3,2,1,0:T(8,128)(2,1)S(1)}, bf16[2,2,128,128]{3,2,1,0:T(8,128)(2,1)S(1)}, u32[]{:S(2)}, u32[]{:S(2)}) collective-permute-start(bf16[2,2,128,128]{3,2,1,0:T(8,128)(2,1)S(1)} %get-tuple-element.15), channel_id=1, source_target_pairs={{0,8},{4,12},{8,0},{12,4},{1,9},{5,13},{9,1},{13,5},{2,10},{6,14},... | collective-permute-start | bytes 393224 | tf_op jit(solution)/shard_map/ppermute | solution.py:195
  35.5 0.7 %collective-permute-start.7 = (bf16[2,2,128,128]{3,2,1,0:T(8,128)(2,1)S(1)}, bf16[2,2,128,128]{3,2,1,0:T(8,128)(2,1)S(1)}, u32[]{:S(2)}, u32[]{:S(2)}) collective-permute-start(bf16[2,2,128,128]{3,2,1,0:T(8,128)(2,1)S(1)} %get-tuple-element.16), channel_id=1, source_target_pairs={{0,12},{4,0},{8,4},{12,8},{1,13},{5,1},{9,5},{13,9},{2,14},{6,2},{... | collective-permute-start | bytes 393224 | tf_op jit(solution)/shard_map/ppermute | solution.py:195
  36.2 0.0 copy-done.4
  36.2 0.0 copy-done.7
  36.2 5.7 %listed_queries.1 = f32[128,32,128]{2,1,0:T(8,128)} custom-call(s32[2]{0:T(128)S(1)} %pad_add_fusion.place_ref, s32[2,8]{1,0:T(2,128)S(1)} %bitcast.11, bf16[2,2,128,128]{3,2,1,0:T(8,128)(2,1)S(1)} %pack.1.kv_ref.refs_0_, bf16[2,2,128,128]{3,2,1,0:T(8,128)(2,1)} %collective-permute-done.refs_1_, bf16[2,2,128,128]{3,2,1,0:T(8,128)(2,1)} %collective-permute-done.1.refs_2_, ...), custom_call_target="tpu_custom_call" | custom-call | flops 805306368 | bytes 6291456 | tf_op jit(solution)/shard_map/listed_queries/pallas_call | solution.py:281
  41.9 0.0 collective-permute-done.5.refs_0_
  42.0 3.4 %collective-permute-done.6.refs_1_ = bf16[2,2,128,128]{3,2,1,0:T(8,128)(2,1)S(1)} collective-permute-done((bf16[2,2,128,128]{3,2,1,0:T(8,128)(2,1)S(1)}, bf16[2,2,128,128]{3,2,1,0:T(8,128)(2,1)S(1)}, u32[]{:S(2)}, u32[]{:S(2)}) %collective-permute-start.6) | collective-permute-done | bytes 131104 | tf_op jit(solution)/shard_map/ppermute | solution.py:195
  45.4 2.5 %collective-permute-done.7.refs_2_ = bf16[2,2,128,128]{3,2,1,0:T(8,128)(2,1)S(1)} collective-permute-done((bf16[2,2,128,128]{3,2,1,0:T(8,128)(2,1)S(1)}, bf16[2,2,128,128]{3,2,1,0:T(8,128)(2,1)S(1)}, u32[]{:S(2)}, u32[]{:S(2)}) %collective-permute-start.7) | collective-permute-done | bytes 131104 | tf_op jit(solution)/shard_map/ppermute | solution.py:195
  47.9 0.8 %total.1 = (f32[128,2,128]{2,1,0:T(2,128)}, f32[128,2,128]{2,1,0:T(2,128)}) custom-call(f32[2,2,128,128]{3,2,1,0:T(8,128)S(1)} %get-tuple-element.11.refs_4_.near_ref, f32[2,2,128,128]{3,2,1,0:T(8,128)S(1)} %get-tuple-element.13.own_ref, bf16[2,2,128,128]{3,2,1,0:T(8,128)(2,1)S(1)} %collective-permute-done.5.refs_0_, ...), custom_call_target="tpu_custom_call" | custom-call | tf_op jit(solution)/shard_map/total/pallas_call | solution.py:293
  (13 shorter events, 0.0 us)
Async XLA Ops:
  0.6 0.8 %copy-start.9 = (bf16[128,2,128]{2,1,0:T(2,128)(2,1)S(1)}, bf16[128,2,128]{2,1,0:T(2,128)(2,1)}, u32[]{:S(2)}) copy-start(bf16[128,2,128]{2,1,0:T(2,128)(2,1)} %key_ref.1) | copy-start | bytes 196612
  1.5 0.8 %copy-start.10 = (bf16[128,2,128]{2,1,0:T(2,128)(2,1)S(1)}, bf16[128,2,128]{2,1,0:T(2,128)(2,1)}, u32[]{:S(2)}) copy-start(bf16[128,2,128]{2,1,0:T(2,128)(2,1)} %value_ref.1) | copy-start | bytes 196612
  2.3 22.7 %copy-start.1 = (bf16[128,32,128]{2,1,0:T(8,128)(2,1)S(1)}, bf16[128,32,128]{2,1,0:T(8,128)(2,1)}, u32[]{:S(2)}) copy-start(bf16[128,32,128]{2,1,0:T(8,128)(2,1)} %refs_5_.3) | copy-start | bytes 3145732
  2.7 17.7 %collective-permute-start.2 = (bf16[2,2,128,128]{3,2,1,0:T(8,128)(2,1)S(1)}, bf16[2,2,128,128]{3,2,1,0:T(8,128)(2,1)}, u32[]{:S(2)}, u32[]{:S(2)}) collective-permute-start(bf16[2,2,128,128]{3,2,1,0:T(8,128)(2,1)S(1)} %pack.1.kv_ref.refs_0_), channel_id=1, source_target_pairs={{0,12},{4,0},{8,4},{12,8},{1,13},{5,1},{9,5},{13,9},{2,14},{6,2},{... | collective-permute-start | bytes 393224 | tf_op jit(solution)/shard_map/ppermute | solution.py:195
  2.7 17.6 %collective-permute-start.1 = (bf16[2,2,128,128]{3,2,1,0:T(8,128)(2,1)S(1)}, bf16[2,2,128,128]{3,2,1,0:T(8,128)(2,1)}, u32[]{:S(2)}, u32[]{:S(2)}) collective-permute-start(bf16[2,2,128,128]{3,2,1,0:T(8,128)(2,1)S(1)} %pack.1.kv_ref.refs_0_), channel_id=1, source_target_pairs={{0,8},{4,12},{8,0},{12,4},{1,9},{5,13},{9,1},{13,5},{2,10},{6,14},... | collective-permute-start | bytes 393224 | tf_op jit(solution)/shard_map/ppermute | solution.py:195
  5.2 15.2 %collective-permute-start = (bf16[2,2,128,128]{3,2,1,0:T(8,128)(2,1)S(1)}, bf16[2,2,128,128]{3,2,1,0:T(8,128)(2,1)}, u32[]{:S(2)}, u32[]{:S(2)}) collective-permute-start(bf16[2,2,128,128]{3,2,1,0:T(8,128)(2,1)S(1)} %pack.1.kv_ref.refs_0_), channel_id=1, source_target_pairs={{0,4},{4,8},{8,12},{12,0},{1,5},{5,9},{9,13},{13,1},{2,6},{6,10},{... | collective-permute-start | bytes 393224 | tf_op jit(solution)/shard_map/ppermute | solution.py:195
  12.7 1.2 %copy-start = (bf16[128,32,128]{2,1,0:T(8,128)(2,1)S(1)}, bf16[128,32,128]{2,1,0:T(8,128)(2,1)}, u32[]{:S(2)}) copy-start(bf16[128,32,128]{2,1,0:T(8,128)(2,1)} %refs_5_.3) | copy-start | bytes 3145732
  13.9 1.2 %copy-start.2 = (bf16[128,32,128]{2,1,0:T(8,128)(2,1)S(1)}, bf16[128,32,128]{2,1,0:T(8,128)(2,1)}, u32[]{:S(2)}) copy-start(bf16[128,32,128]{2,1,0:T(8,128)(2,1)} %refs_6_.3) | copy-start | bytes 3145732
  15.2 0.7 %copy-start.5 = (f32[2,1,2048]{2,1,0:T(1,128)S(1)}, f32[2,1,2048]{2,1,0:T(1,128)}, u32[]{:S(2)}) copy-start(f32[2,1,2048]{2,1,0:T(1,128)} %reshape.27.term_ref.refs_8_) | copy-start | bytes 49156
  15.9 0.8 %copy-start.8 = (s32[128,1]{1,0:T(8,128)S(1)}, s32[128,1]{1,0:T(8,128)}, u32[]{:S(2)}) copy-start(s32[128,1]{1,0:T(8,128)} %copy.18.doc_col_ref) | copy-start | bytes 1540
  16.7 0.7 %copy-start.14 = (s32[1,2048]{1,0:T(1,128)S(1)}, s32[1,2048]{1,0:T(1,128)}, u32[]{:S(2)}) copy-start(s32[1,2048]{1,0:T(1,128)} %reshape_reshape.3.docs_ref) | copy-start | bytes 24580
  20.4 0.7 %copy-start.11 = (s32[8,2]{0,1:T(2,128)S(1)}, s32[8,2]{0,1:T(2,128)}, u32[]{:S(2)}) copy-start(s32[8,2]{0,1:T(2,128)} %param.15) | copy-start | bytes 196
  21.1 12.0 %copy-start.13 = (s32[8,2]{0,1:T(2,128)S(1)}, s32[8,2]{0,1:T(2,128)}, u32[]{:S(2)}) copy-start(s32[8,2]{0,1:T(2,128)} %param.15) | copy-start | bytes 196
  21.1 15.1 %copy-start.4 = (bf16[128,32,128]{2,1,0:T(8,128)(2,1)S(1)}, bf16[128,32,128]{2,1,0:T(8,128)(2,1)}, u32[]{:S(2)}) copy-start(bf16[128,32,128]{2,1,0:T(8,128)(2,1)} %refs_6_.3) | copy-start | bytes 3145732
  22.3 2.7 %collective-permute-start.3 = (bf16[2,2,2,128,128]{4,3,2,1,0:T(8,128)(2,1)S(1)}, bf16[2,2,2,128,128]{4,3,2,1,0:T(8,128)(2,1)S(1)}, u32[]{:S(2)}, u32[]{:S(2)}) collective-permute-start(bf16[2,2,2,128,128]{4,3,2,1,0:T(8,128)(2,1)S(1)} %choose.1), channel_id=1, source_target_pairs={{0,1},{1,0},{2,3},{3,2},{4,5},{5,4},{6,7},{7,6},{8,9},{9,8},{10,11... | collective-permute-start | bytes 786440 | tf_op jit(solution)/shard_map/ppermute | solution.py:198
  25.0 1.2 %copy-start.3 = (bf16[128,32,128]{2,1,0:T(8,128)(2,1)S(1)}, bf16[128,32,128]{2,1,0:T(8,128)(2,1)}, u32[]{:S(2)}) copy-start(bf16[128,32,128]{2,1,0:T(8,128)(2,1)} %refs_6_.3) | copy-start | bytes 3145732
  26.3 0.7 %copy-start.6 = (f32[2,1,2048]{2,1,0:T(1,128)S(1)}, f32[2,1,2048]{2,1,0:T(1,128)}, u32[]{:S(2)}) copy-start(f32[2,1,2048]{2,1,0:T(1,128)} %reshape.27.term_ref.refs_8_) | copy-start | bytes 49156
  27.0 0.7 %copy-start.12 = (s32[8,2]{0,1:T(2,128)S(1)}, s32[8,2]{0,1:T(2,128)}, u32[]{:S(2)}) copy-start(s32[8,2]{0,1:T(2,128)} %param.15) | copy-start | bytes 196
  27.6 8.6 %copy-start.7 = (f32[2,1,2048]{2,1,0:T(1,128)S(1)}, f32[2,1,2048]{2,1,0:T(1,128)}, u32[]{:S(2)}) copy-start(f32[2,1,2048]{2,1,0:T(1,128)} %reshape.27.term_ref.refs_8_) | copy-start | bytes 49156
  31.5 1.6 %collective-permute-start.4 = (bf16[2,2,2,128,128]{4,3,2,1,0:T(8,128)(2,1)S(1)}, bf16[2,2,2,128,128]{4,3,2,1,0:T(8,128)(2,1)S(1)}, u32[]{:S(2)}, u32[]{:S(2)}) collective-permute-start(bf16[2,2,2,128,128]{4,3,2,1,0:T(8,128)(2,1)S(1)} %listed_keys.1.mine_ref), channel_id=1, source_target_pairs={{0,1},{1,0},{2,3},{3,2},{4,5},{5,4},{6,7},{7,6},{8,9},{9,8},{10,11... | collective-permute-start | bytes 786440 | tf_op jit(solution)/shard_map/ppermute | solution.py:198
  34.1 7.9 %collective-permute-start.5 = (bf16[2,2,128,128]{3,2,1,0:T(8,128)(2,1)S(1)}, bf16[2,2,128,128]{3,2,1,0:T(8,128)(2,1)S(1)}, u32[]{:S(2)}, u32[]{:S(2)}) collective-permute-start(bf16[2,2,128,128]{3,2,1,0:T(8,128)(2,1)S(1)} %get-tuple-element.14), channel_id=1, source_target_pairs={{0,4},{4,8},{8,12},{12,0},{1,5},{5,9},{9,13},{13,1},{2,6},{6,10},{... | collective-permute-start | bytes 393224 | tf_op jit(solution)/shard_map/ppermute | solution.py:195
  34.1 11.2 %collective-permute-start.6 = (bf16[2,2,128,128]{3,2,1,0:T(8,128)(2,1)S(1)}, bf16[2,2,128,128]{3,2,1,0:T(8,128)(2,1)S(1)}, u32[]{:S(2)}, u32[]{:S(2)}) collective-permute-start(bf16[2,2,128,128]{3,2,1,0:T(8,128)(2,1)S(1)} %get-tuple-element.15), channel_id=1, source_target_pairs={{0,8},{4,12},{8,0},{12,4},{1,9},{5,13},{9,1},{13,5},{2,10},{6,14},... | collective-permute-start | bytes 393224 | tf_op jit(solution)/shard_map/ppermute | solution.py:195
  35.5 12.4 %collective-permute-start.7 = (bf16[2,2,128,128]{3,2,1,0:T(8,128)(2,1)S(1)}, bf16[2,2,128,128]{3,2,1,0:T(8,128)(2,1)S(1)}, u32[]{:S(2)}, u32[]{:S(2)}) collective-permute-start(bf16[2,2,128,128]{3,2,1,0:T(8,128)(2,1)S(1)} %get-tuple-element.16), channel_id=1, source_target_pairs={{0,12},{4,0},{8,4},{12,8},{1,13},{5,1},{9,5},{13,9},{2,14},{6,2},{... | collective-permute-start | bytes 393224 | tf_op jit(solution)/shard_map/ppermute | solution.py:195
